TPU v7x, 128 devices: a whole 4x4x4 slice. The times are simulated.
128 devices in a mesh: ctx: 4 (over y), exp: 32 (over z, x, core).
Axes of the slice: x: 4, y: 4, z: 4, core: 2. Of those that a mesh axis runs over, the one named last changes fastest.
Arguments:
- queries: bfloat16 [4096, 2, 4096], P('ctx', None, 'exp'), may hold values from -8 to 8
- key_rows: bfloat16 [4096, 2, 256], P(('ctx', 'exp')), may hold values from -8 to 8
- values: bfloat16 [4096, 2, 256], P(('ctx', 'exp')), may hold values from -6 to 6
- hidden: bfloat16 [4096, 2, 4096], P(('ctx', 'exp')), may hold values from -6 to 6
- norm_gain: float32 [4096], replicated, may hold values from 0.5 to 2
- routes: int32 [4096, 2, 8], P(('ctx', 'exp')), may hold values from 0 to 127, all different within a row
- route_gates: float32 [4096, 2, 8], P(('ctx', 'exp')), may hold values from 0.02 to 0.3
- expert_home: int32 [128], replicated, may hold values from 0 to 127, each once
- w_gate: bfloat16 [128, 4096, 768], P(('ctx', 'exp')), may hold values from -0.09375 to 0.09375
- w_up: bfloat16 [128, 4096, 768], P(('ctx', 'exp')), may hold values from -0.09375 to 0.09375
- w_down: bfloat16 [128, 768, 4096], P(('ctx', 'exp')), may hold values from -0.21875 to 0.21875
Outputs:
- context: bfloat16 [4096, 2, 4096], P('ctx', None, 'exp')
- layer_out: bfloat16 [4096, 2, 4096], P(('ctx', 'exp'))
Inputs may be any that keep to these rules, and one draw needn't show every extreme that they name: `routes`: each token names 8 different experts. `expert_home`: a permutation of the 128 experts.
All inputs are finite; a program needn't handle non-finite values.
Results may differ from a plain program's by a relative error of at most 0.0045.
Values may be sent and summed in bfloat16 or wider, within the bound.
A program may use at most 128 MiB of HBM per device.

v0:
```python
from functools import partial

import jax
import jax.numpy as jnp
from jax import lax
from jax.sharding import PartitionSpec as P

QUERY_HEADS = 32
KEY_VALUE_HEADS = 2
HEAD_WIDTH = 128
TOPK = 8
SEQUENCE_COUNT = 2


neg_fill = -1e30


def from_behind(value, axis, steps):
    count = lax.axis_size(axis)
    first, last = (max(0, -steps), min(count, count - steps))
    return lax.ppermute(value, axis, [(source, source + steps) for source in range(first, last)])


def empty_running(query_rows, heads_per_shard):
    array_shape = (query_rows, SEQUENCE_COUNT, heads_per_shard)
    return (
        jnp.full(array_shape, neg_fill, jnp.float32),
        jnp.zeros(array_shape, jnp.float32),
        jnp.zeros(array_shape + (HEAD_WIDTH,), jnp.float32),
    )


def keep_same(running):
    return running


def absorb(query_heads, query_pos, key_value, key_pos, running):
    scores = jnp.einsum(
        "cshd,ksd->cshk", query_heads, key_value[0], preferred_element_type=jnp.float32
    ) * HEAD_WIDTH ** (-0.5)
    visible = key_pos[None, None, None, :] <= query_pos[:, None, None, None]
    scores = jnp.where(visible, scores, neg_fill)
    best_old, total_old, accum_old = running
    best_new = jnp.maximum(best_old, jnp.max(scores, axis=-1))
    weights = jnp.where(visible, jnp.exp(scores - best_new[..., None]), 0.0)
    factor = jnp.exp(best_old - best_new)
    total_new = total_old * factor + jnp.sum(weights, axis=-1)
    attended = jnp.einsum(
        "cshk,ksd->cshd",
        weights.astype(jnp.bfloat16),
        key_value[1],
        preferred_element_type=jnp.float32,
    )
    return (best_new, total_new, accum_old * factor[..., None] + attended)


def finish(states, feature_width):
    parts = [state_item[2] / state_item[1][..., None] for state_item in states]
    joined = parts[0]
    return joined.reshape(joined.shape[0], SEQUENCE_COUNT, feature_width).astype(jnp.bfloat16)


def expert_rows(gate_rows, up_rows, down_rows, rows_in):
    tokens_flat = rows_in.reshape(-1, rows_in.shape[-1])
    gate_proj = jnp.dot(tokens_flat, gate_rows, preferred_element_type=jnp.float32)
    up_proj = jnp.dot(tokens_flat, up_rows, preferred_element_type=jnp.float32)
    active = (jax.nn.silu(gate_proj) * up_proj).astype(jnp.bfloat16)
    produced = jnp.dot(active, down_rows, preferred_element_type=jnp.float32).astype(jnp.bfloat16)
    return produced.reshape(rows_in.shape)


def body(
    queries,
    key_rows,
    values,
    hidden,
    norm_gain,
    routes,
    route_gates,
    expert_home,
    w_gate,
    w_up,
    w_down,
):
    ctx_count = lax.axis_size("ctx")
    exp_count = lax.axis_size("exp")
    ctx_index = lax.axis_index("ctx")
    expert_position = lax.axis_index("exp")
    block_rows = queries.shape[0]
    feature_width = queries.shape[2]
    heads_per_shard = feature_width // HEAD_WIDTH
    query_heads = queries.reshape(block_rows, SEQUENCE_COUNT, heads_per_shard, HEAD_WIDTH)
    key_full, value_full = (
        lax.all_gather(key_rows, "exp", axis=0, tiled=True),
        lax.all_gather(values, "exp", axis=0, tiled=True),
    )
    key_value_head = expert_position * heads_per_shard // (QUERY_HEADS // KEY_VALUE_HEADS)
    own_keys = lax.dynamic_slice_in_dim(key_full, key_value_head * HEAD_WIDTH, HEAD_WIDTH, 2)
    own_values = lax.dynamic_slice_in_dim(value_full, key_value_head * HEAD_WIDTH, HEAD_WIDTH, 2)
    key_value = jnp.stack([own_keys, own_values])
    rows_local = jnp.arange(block_rows, dtype=jnp.int32)
    own_pos = ctx_index * block_rows + rows_local
    running = absorb(
        query_heads, own_pos, key_value, own_pos, empty_running(block_rows, heads_per_shard)
    )
    moving = key_value
    for hop_count in range(1, ctx_count):
        moving = from_behind(moving, "ctx", 1)
        source = ctx_index - hop_count
        running = lax.cond(
            source >= 0,
            partial(absorb, query_heads, own_pos, moving, source * block_rows + rows_local),
            keep_same,
            running,
        )
    context = finish((running,), feature_width)
    token_count = hidden.shape[0] * hidden.shape[1]
    model_width = hidden.shape[2]
    device_count = ctx_count * exp_count
    expert_count = expert_home.shape[0]
    capacity = max(2, 3 * token_count * TOPK // (4 * expert_count))
    tokens_flat = hidden.reshape(token_count, model_width).astype(jnp.float32)
    normed = (
        tokens_flat
        * lax.rsqrt(jnp.mean(tokens_flat * tokens_flat, axis=-1, keepdims=True) + 1e-06)
        * norm_gain
    ).astype(jnp.bfloat16)
    chosen = routes.reshape(token_count, TOPK)
    gate_values = route_gates.reshape(token_count, TOPK)
    expert_ids = jnp.arange(expert_count, dtype=jnp.int32)
    picked = chosen[:, :, None] == expert_ids[None, None, :]
    per_token = jnp.sum(picked, axis=1).astype(jnp.float32)
    token_ids = jnp.arange(token_count, dtype=jnp.int32)
    earlier = (token_ids[None, :] < token_ids[:, None]).astype(jnp.float32)
    before = jnp.dot(earlier, per_token, precision=lax.Precision.HIGHEST)
    slot_rank = jnp.sum(jnp.where(picked, before[:, None, :], 0.0), axis=-1).astype(jnp.int32)
    home_of = jnp.sum(jnp.where(picked, expert_home[None, None, :], 0), axis=-1)
    slot_index = jnp.where(slot_rank < capacity, home_of * capacity + slot_rank, -1)
    slot_ids = jnp.arange(device_count * capacity, dtype=jnp.int32)
    placing = jnp.any(slot_index[None, :, :] == slot_ids[:, None, None], axis=-1).astype(
        jnp.bfloat16
    )
    outgoing = jnp.dot(placing, normed, preferred_element_type=jnp.float32).astype(jnp.bfloat16)
    run_expert = partial(expert_rows, w_gate[0], w_up[0], w_down[0])
    sending = outgoing.reshape(device_count, capacity, model_width)
    processed = run_expert(
        lax.all_to_all(sending, ("ctx", "exp"), split_axis=0, concat_axis=0, tiled=True)
    )
    returned = lax.all_to_all(processed, ("ctx", "exp"), split_axis=0, concat_axis=0, tiled=True)
    returned = returned.reshape(device_count * capacity, model_width)
    gathered = jnp.take(returned, jnp.maximum(slot_index, 0), axis=0)
    kept_gates = jnp.where(slot_index >= 0, gate_values, 0.0)
    combined = jnp.einsum(
        "tk,tkd->td", kept_gates, gathered.astype(jnp.float32), precision=lax.Precision.HIGHEST
    )
    layer_out = (tokens_flat + combined).astype(jnp.bfloat16).reshape(hidden.shape)
    return (context, layer_out)


def solution(mesh):
    in_specs = (
        P("ctx", None, "exp"),
        P(("ctx", "exp"), None, None),
        P(("ctx", "exp"), None, None),
        P(("ctx", "exp"), None, None),
        P(),
        P(("ctx", "exp"), None, None),
        P(("ctx", "exp"), None, None),
        P(),
        P(("ctx", "exp"), None, None),
        P(("ctx", "exp"), None, None),
        P(("ctx", "exp"), None, None),
    )
    out_specs = (P("ctx", None, "exp"), P(("ctx", "exp"), None, None))
    return jax.shard_map(body, mesh=mesh, in_specs=in_specs, out_specs=out_specs, check_vma=False)
```

profile of v0, /device:TPU:60, one launch (start us, length us, event | category | flops | bytes accessed | tf_op | source)
XLA Modules:
  0.0 321.3 jit_solution(9744476034995325928)
XLA Ops:
  7.2 0.0 all-gather.5.cloned.1.call-start
  7.2 0.7 all-gather.5.cloned.1.call-update
  7.9 0.0 all-gather.3.cloned.1.call-start
  7.9 1.4 copy.58
  9.3 0.0 all-gather.3.cloned.1.call-update
  9.3 2.2 reshape.359
  11.5 1.7 multiply_reduce_fusion
  13.2 0.8 copy.68
  14.0 1.9 convert_reduce_fusion
  15.9 0.1 fusion.113
  16.0 0.2 select_reduce_fusion.1
  16.3 0.3 fusion.102
  16.6 0.1 rsqrt.12
  16.7 2.3 convolution_convert_fusion
  19.0 4.5 %reshape.354 = bf16[128,3,4096]{2,1,0:T(4,128)(2,1)} reshape(bf16[384,4096]{1,0:T(8,128)(2,1)S(1)} %convolution_convert_fusion) | data formatting | bytes 6291456 | tf_op jit(solution)/shard_map/reshape | solution.py:145
  23.5 10.5 %all-to-all-start = ((bf16[128,3,4096]{2,1,0:T(4,128)(2,1)}), bf16[128,3,4096]{2,1,0:T(4,128)(2,1)}, u32[]{:S(2)}, u32[]{:S(2)}) async-start(bf16[128,3,4096]{2,1,0:T(4,128)(2,1)} %reshape.354), calls=%async_computation | async-start | bytes 8388608 | tf_op jit(solution)/shard_map/all_to_all | solution.py:147
  34.0 0.9 copy.90
  34.9 52.7 %all-gather.5.cloned.1.call-done = bf16[1024,2,256]{2,1,0:T(2,128)(2,1)} async-done(((bf16[32,2,256]{2,1,0:T(2,128)(2,1)}), bf16[1024,2,256]{2,1,0:T(2,128)(2,1)}) %all-gather.5.cloned.1.call-update) | async-done | bytes 1048592 | tf_op jit(solution)/shard_map/all_gather | solution.py:95
  87.6 1.4 constant_dynamic-slice_fusion
  89.0 0.1 copy.89
  89.0 43.6 %all-gather.3.cloned.1.call-done = bf16[1024,2,256]{2,0,1:T(8,128)(2,1)} async-done(((bf16[32,2,256]{2,0,1:T(8,128)(2,1)}), bf16[1024,2,256]{2,0,1:T(8,128)(2,1)}) %all-gather.3.cloned.1.call-update) | async-done | bytes 1048592 | tf_op jit(solution)/shard_map/all_gather | solution.py:94
  132.6 1.1 dynamic-slice_bitcast_fusion
  133.7 0.1 pad_maximum_fusion
  133.8 1.3 collective-permute-start
  135.1 0.1 reshape.362
  135.2 0.1 copy.69
  135.4 0.7 broadcast_compare_fusion.3
  136.0 25.1 %collective-permute-done = bf16[2,1024,2,128]{3,1,2,0:T(8,128)(2,1)} collective-permute-done((bf16[2,1024,2,128]{3,1,2,0:T(8,128)(2,1)S(1)}, bf16[2,1024,2,128]{3,1,2,0:T(8,128)(2,1)}, u32[]{:S(2)}, u32[]{:S(2)}) %collective-permute-start) | collective-permute-done | bytes 1048608 | tf_op jit(solution)/shard_map/ppermute | solution.py:21
  161.1 1.5 collective-permute-start.1
  162.6 0.0 all-to-all-done
  162.6 7.4 %reshape.355 = bf16[384,4096]{1,0:T(8,128)(2,1)} reshape(bf16[128,3,4096]{2,1,0:T(4,128)(2,1)} %all-to-all-done) | data formatting | bytes 6291456 | tf_op jit(solution)/shard_map/reshape | solution.py:64
  170.0 7.4 %fusion.75 = f32[384,768]{1,0:T(8,128)} fusion(bf16[384,4096]{1,0:T(8,128)(2,1)} %reshape.355, bf16[1,4096,768]{2,1,0:T(8,128)(2,1)} %param.25), kind=kOutput, calls=%fused_computation.83 | convolution fusion | flops 2415919104 | bytes 10616832 | tf_op jit(solution)/shard_map/dot_general | solution.py:65
  177.4 14.2 %fusion.79 = bf16[384,4096]{1,0:T(8,128)(2,1)} fusion(bf16[1,768,4096]{2,1,0:T(8,128)(2,1)} %param.27, bf16[384,4096]{1,0:T(8,128)(2,1)} %reshape.355, bf16[1,4096,768]{2,1,0:T(8,128)(2,1)} %param.26, f32[384,768]{1,0:T(8,128)} %fusion.75), kind=kOutput, calls=%fused_computation.88 | convolution fusion | flops 4835180544 | bytes 20054016 | tf_op jit(solution)/shard_map/dot_general | solution.py:68
  191.6 7.2 %reshape.356 = bf16[128,3,4096]{2,1,0:T(4,128)(2,1)} reshape(bf16[384,4096]{1,0:T(8,128)(2,1)} %fusion.79) | data formatting | bytes 6291456 | tf_op jit(solution)/shard_map/reshape | solution.py:69
  198.8 11.8 %all-to-all-start.1 = ((bf16[128,3,4096]{2,1,0:T(4,128)(2,1)}), bf16[128,3,4096]{2,1,0:T(4,128)(2,1)}, u32[]{:S(2)}, u32[]{:S(2)}) async-start(bf16[128,3,4096]{2,1,0:T(4,128)(2,1)} %reshape.356), calls=%async_computation.1 | async-start | bytes 8388608 | tf_op jit(solution)/shard_map/all_to_all | solution.py:149
  210.6 1.8 fusion.70
  212.4 2.3 fusion.78
  214.7 1.5 collective-permute-start.2
  216.3 2.9 fusion.95
  219.2 17.7 %conditional.3 = (f32[1024,2,1]{0,1,2:T(2,128)S(1)}, f32[1024,2,1]{0,1,2:T(2,128)S(1)}, f32[1024,2,1,128]{3,0,1,2:T(8,128)S(1)}) conditional(s32[]{:T(128)} %convert_element_type.79, (f32[1024,2,1]{0,1,2:T(2,128)S(1)}, f32[1024,2,1]{0,1,2:T(2,128)S(1)}, f32[1024,2,1,128]{0,3,1,2:T(8,128)S(1)}) %tuple.28, (s32[1024]{0:T(1024)S(1)}, ...), branch_computations={%region_2.3_spmd, %region_3.6_spmd} | conditional | flops 1102583808 | bytes 68821048 | solution.py:110
  219.2 0.7 broadcast_compare_fusion
  219.8 6.2 %fusion = (f32[1024,2]{0,1:T(2,128)S(1)}, f32[2,1024,1024]{2,1,0:T(8,128)}) fusion(pred[1024,1024]{0,1:T(8,128)(4,1)S(1)} %broadcast_compare_fusion, bf16[1024,2,1,128]{3,0,1,2:T(8,128)(2,1)} %get-tuple-element.74, bf16[2,1024,2,128]{3,1,2,0:T(8,128)(2,1)} %get-tuple-element.73), kind=kOutput, calls=%fused_computation.3 | convolution fusion | flops 543160320 | bytes 10493952 | tf_op jit(solution)/shard_map/cond/branch_1_fun/cshd,ksd->cshk/dot_general | solution.py:38
  226.1 1.3 copy.65
  227.4 7.2 %fusion.10 = f32[1024,2,1,128]{3,0,1,2:T(8,128)S(1)} fusion(f32[2,1024,1024]{2,1,0:T(8,128)} %get-tuple-element.167, f32[1024,2]{0,1:T(2,128)S(1)} %bitcast.261, pred[1024,1024]{0,1:T(8,128)(4,1)S(1)} %broadcast_compare_fusion, f32[1024,2,1,128]{3,0,1,2:T(8,128)} %copy.65, bf16[2,1024,2,128]{3,1,2,0:T(8,128)(2,1)} %get-tuple-element.73, ...), kind=kOutput, calls=%fused_computation.11 | convolution fusion | flops 547880960 | bytes 12075008 | tf_op jit(solution)/shard_map/cond/branch_1_fun/cshk,ksd->cshd/dot_general | solution.py:48
  234.6 2.3 fusion.2
  236.9 11.2 %conditional.4 = ((f32[1024,2,1]{0,1,2:T(2,128)S(1)}, f32[1024,2,1]{0,1,2:T(2,128)S(1)}, f32[1024,2,1,128]{3,0,1,2:T(8,128)S(1)})) conditional(s32[]{:T(128)} %convert_element_type.78, (f32[1024,2,1]{0,1,2:T(2,128)S(1)}, f32[1024,2,1]{0,1,2:T(2,128)S(1)}, f32[1024,2,1,128]{3,0,1,2:T(8,128)S(1)}) %conditional.3, (s32[]{:T(128)}, s32[1024]{0:T(1024)S(1)}, ...), branch_computations={%region_6.7_spmd, %region_7.10_spmd} | conditional | flops 1102584832 | bytes 33177648 | solution.py:110
  237.4 0.7 broadcast_compare_fusion.1
  238.0 3.0 fusion.23
  241.1 2.3 fusion.25
  243.4 4.7 %fusion.33 = f32[1024,2,1,128]{3,0,1,2:T(8,128)S(1)} fusion(f32[2,1024,1024]{2,1,0:T(8,128)S(1)} %get-tuple-element.169, f32[1024,2]{0,1:T(2,128)S(1)} %bitcast.264, pred[1024,1024]{0,1:T(8,128)(4,1)S(1)} %broadcast_compare_fusion.1, f32[1024,2,1,128]{3,0,1,2:T(8,128)S(1)} %get-tuple-element.84, bf16[2,1024,2,128]{3,1,2,0:T(8,128)(2,1)} %get-tuple-element.81, ...), kind=kOutput, calls=%fused_computation.35 | convolution fusion | flops 547880960 | bytes 12075008 | tf_op jit(solution)/shard_map/cond/branch_1_fun/cshk,ksd->cshd/dot_general | solution.py:48
  248.1 31.8 %collective-permute-done.2 = bf16[2,1024,2,128]{3,1,2,0:T(8,128)(2,1)} collective-permute-done((bf16[2,1024,2,128]{3,1,2,0:T(8,128)(2,1)}, bf16[2,1024,2,128]{3,1,2,0:T(8,128)(2,1)}, u32[]{:S(2)}, u32[]{:S(2)}) %collective-permute-start.2) | collective-permute-done | bytes 1048608 | tf_op jit(solution)/shard_map/ppermute | solution.py:21
  280.0 11.9 %conditional.5 = (f32[1024,2,1]{0,1,2:T(2,128)S(1)}, f32[1024,2,1,128]{3,1,0,2:T(2,128)S(1)}) conditional(s32[]{:T(128)} %convert_element_type.77, (f32[1024,2,1]{0,1,2:T(2,128)S(1)}, f32[1024,2,1,128]{3,0,1,2:T(8,128)S(1)}) %tuple.31, (s32[]{:T(128)}, s32[1024]{0:T(1024)S(1)}, s32[1024]{0:T(1024)S(1)}, bf16[2,1024,2,128]{3,1,2,0:T(8,128)(2,1)}, ...), branch_computations={%region_10.11_spmd, %region_11.14_spmd} | conditional | flops 1102584832 | bytes 35258400 | solution.py:110
  280.1 0.7 broadcast_compare_fusion.2
  280.8 3.0 fusion.46
  283.8 2.3 fusion.48
  286.1 4.7 %fusion.56 = f32[1024,2,1,128]{3,0,1,2:T(8,128)S(1)} fusion(f32[2,1024,1024]{2,1,0:T(8,128)S(1)} %get-tuple-element.165, f32[1024,2]{0,1:T(2,128)S(1)} %fusion.65, pred[1024,1024]{0,1:T(8,128)(4,1)S(1)} %broadcast_compare_fusion.2, f32[1024,2,1,128]{3,0,1,2:T(8,128)S(1)} %get-tuple-element.92, bf16[2,1024,2,128]{3,1,2,0:T(8,128)(2,1)} %get-tuple-element.90, ...), kind=kOutput, calls=%fused_computation.60 | convolution fusion | flops 547880960 | bytes 12075008 | tf_op jit(solution)/shard_map/cond/branch_1_fun/cshk,ksd->cshd/dot_general | solution.py:48
  290.9 0.8 copy.77
  291.9 0.2 copy.66
  292.1 3.1 fusion.108
  295.2 6.0 %reshape.357 = bf16[384,4096]{1,0:T(8,128)(2,1)S(1)} reshape(bf16[128,3,4096]{2,1,0:T(4,128)(2,1)} %all-to-all-done.1) | data formatting | bytes 6291456 | tf_op jit(solution)/shard_map/reshape | solution.py:150
  301.2 4.4 %gather_fusion = bf16[512,4096]{1,0:T(8,128)(2,1)} fusion(bf16[384,4096]{1,0:T(8,128)(2,1)S(1)} %reshape.357, s32[1024]{0:T(1024)S(1)} %pad_clamp_fusion), kind=kCustom, calls=%fused_computation | custom fusion | bytes 8390656 | tf_op jit(solution)/shard_map/jit(_take)/gather | solution.py:151
  305.6 5.7 %fusion.83 = f32[64,1,4096]{2,1,0:T(1,128)S(1)} fusion(f32[64,8,1]{1,2,0:T(1,128)S(1)} %bitcast.266, bf16[512,4096]{1,0:T(8,128)(2,1)} %gather_fusion, pred[64,8]{1,0:T(8,128)(4,1)S(1)} %get-tuple-element.160), kind=kOutput, calls=%fused_computation.91 | convolution fusion | flops 27262976 | bytes 5245440 | tf_op jit(solution)/shard_map/tk,tkd->td/dot_general | solution.py:153
  311.3 1.9 fusion.101
  313.1 1.1 reshape.358
  (31 shorter events, 0.2 us)
Async XLA Ops:
  7.2 80.4 %all-gather.5.cloned.1.call-start = ((), (), s32[]{:S(2)}) async-start(), calls=%async_computation.3 | async-start | bytes 1081344 | tf_op jit(solution)/shard_map/all_gather | solution.py:95
  7.9 124.7 %all-gather.3.cloned.1.call-start = ((), (), s32[]{:S(2)}) async-start(), calls=%async_computation.2 | async-start | bytes 1081344 | tf_op jit(solution)/shard_map/all_gather | solution.py:94
  23.5 10.6 %copy-start.1 = (bf16[1024,2,128]{2,1,0:T(2,128)(2,1)S(1)}, bf16[1024,2,128]{2,1,0:T(2,128)(2,1)}, u32[]{:S(2)}) copy-start(bf16[1024,2,128]{2,1,0:T(2,128)(2,1)} %param.17) | copy-start | bytes 1572868
  23.5 111.7 %copy-start.3 = (f32[32,2,8]{0,2,1:T(8,128)S(1)}, f32[32,2,8]{0,2,1:T(8,128)}, u32[]{:S(2)}) copy-start(f32[32,2,8]{0,2,1:T(8,128)} %param.23) | copy-start | bytes 6148
  23.5 139.1 %all-to-all-start = ((bf16[128,3,4096]{2,1,0:T(4,128)(2,1)}), bf16[128,3,4096]{2,1,0:T(4,128)(2,1)}, u32[]{:S(2)}, u32[]{:S(2)}) async-start(bf16[128,3,4096]{2,1,0:T(4,128)(2,1)} %reshape.354), calls=%async_computation | async-start | bytes 8388608 | tf_op jit(solution)/shard_map/all_to_all | solution.py:147
  133.8 27.3 %collective-permute-start = (bf16[2,1024,2,128]{3,1,2,0:T(8,128)(2,1)S(1)}, bf16[2,1024,2,128]{3,1,2,0:T(8,128)(2,1)}, u32[]{:S(2)}, u32[]{:S(2)}) collective-permute-start(bf16[2,1024,2,128]{3,1,2,0:T(8,128)(2,1)S(1)} %pad_maximum_fusion), channel_id=1, source_target_pairs={{0,32},{32,64},{64,96},{1,33},{33,65},{65,97},{2,34},{34,66},{66,9... | collective-permute-start | bytes 3145736 | tf_op jit(solution)/shard_map/ppermute | solution.py:21
  161.1 53.6 %collective-permute-start.1 = (bf16[2,1024,2,128]{3,1,2,0:T(8,128)(2,1)}, bf16[2,1024,2,128]{3,1,2,0:T(8,128)(2,1)}, u32[]{:S(2)}, u32[]{:S(2)}) collective-permute-start(bf16[2,1024,2,128]{3,1,2,0:T(8,128)(2,1)} %collective-permute-done), channel_id=1, source_target_pairs={{0,32},{32,64},{64,96},{1,33},{33,65},{65,97},{2,34},{34,66},{66,9... | collective-permute-start | bytes 3145736 | tf_op jit(solution)/shard_map/ppermute | solution.py:21
  191.6 19.0 %copy-start.2 = (bf16[1024,2,256]{2,0,1:T(8,128)(2,1)S(1)}, bf16[1024,2,256]{2,0,1:T(8,128)(2,1)}, u32[]{:S(2)}) copy-start(bf16[1024,2,256]{2,0,1:T(8,128)(2,1)} %all-gather.3.cloned.1.call-done) | copy-start | bytes 3145732
  198.8 96.5 %all-to-all-start.1 = ((bf16[128,3,4096]{2,1,0:T(4,128)(2,1)}), bf16[128,3,4096]{2,1,0:T(4,128)(2,1)}, u32[]{:S(2)}, u32[]{:S(2)}) async-start(bf16[128,3,4096]{2,1,0:T(4,128)(2,1)} %reshape.356), calls=%async_computation.1 | async-start | bytes 8388608 | tf_op jit(solution)/shard_map/all_to_all | solution.py:149
  214.7 65.2 %collective-permute-start.2 = (bf16[2,1024,2,128]{3,1,2,0:T(8,128)(2,1)}, bf16[2,1024,2,128]{3,1,2,0:T(8,128)(2,1)}, u32[]{:S(2)}, u32[]{:S(2)}) collective-permute-start(bf16[2,1024,2,128]{3,1,2,0:T(8,128)(2,1)} %collective-permute-done.1), channel_id=1, source_target_pairs={{0,32},{32,64},{64,96},{1,33},{33,65},{65,97},{2,34},{34,66},{66,9... | collective-permute-start | bytes 3145736 | tf_op jit(solution)/shard_map/ppermute | solution.py:21
  227.4 7.2 %copy-start = (f32[2,1024,1024]{2,1,0:T(8,128)S(1)}, f32[2,1024,1024]{2,1,0:T(8,128)}, u32[]{:S(2)}) copy-start(f32[2,1024,1024]{2,1,0:T(8,128)} %get-tuple-element.167) | copy-start | bytes 25165828 | tf_op jit(solution)/shard_map/cond
Sparse Core Ops, SparseCore 0:
  10.3 77.2 all-gather.4
  90.4 42.1 all-gather.2
where the time goes:
time: 327 us; the launch traced here: 321 us
  waiting for transfers between devices  154 us (47%)
  matrix products  63.4 us (19%)
  local copies, waits for them, and re-layouts  40.9 us (13%)
  starting transfers between devices  26.6 us (8%)
  other arithmetic  21 us (6%)
  between operations  14.6 us (4%)
    ppermute x3, waiting for transfers between devices, from_behind(): lax.ppermute(value, axis, [(source, source + steps) for source in range(f...  57 us
    all_gather x1, waiting for transfers between devices, body(): lax.all_gather(values, 'exp', axis=0, tiled=True)  52.7 us
    all_gather x1, waiting for transfers between devices, body(): lax.all_gather(key_rows, 'exp', axis=0, tiled=True)  43.6 us
    dot_general x4, matrix products, absorb(): jnp.einsum('cshk,ksd->cshd', weights.astype(jnp.bfloat16), key_value[1],...  19.6 us
    dot_general x1, matrix products, expert_rows(): jnp.dot(active, down_rows, preferred_element_type=jnp.float32)  14.2 us
    dot_general x4, matrix products, absorb(): jnp.einsum('cshd,ksd->cshk', query_heads, key_value[0], preferred_element...  14.1 us
    all_to_all x1, starting transfers between devices, body(): lax.all_to_all(processed, ('ctx', 'exp'), split_axis=0, concat_axis=0, ti...  11.8 us
    all_to_all x1, starting transfers between devices, body(): lax.all_to_all(sending, ('ctx', 'exp'), split_axis=0, concat_axis=0, tile...  10.5 us
  transfers between devices with their start and end apart: 7, of which 4 were waited for; matrix products, arithmetic and copies ran while one was open for 33% of the time, Pallas kernels for 0%

commit v1 on v0

v1 whole, which is shorter than its diff:
```python
import jax
import jax.numpy as jnp
import numpy as np
from jax import lax
from jax.experimental import pallas as pl
from jax.experimental.pallas import tpu as pltpu
from jax.sharding import PartitionSpec as P

MESH = pl.DeviceIdType.MESH
HEAD_WIDTH = 128
TOPK = 8
WIDTH = 4096
FF = 768
CAP = 3
TOKENS = 64
SLOTS = 384
CHUNKS = 8
CHUNK = WIDTH // CHUNKS
BLOCK = 1024
ORDERS = (("y", "z", "w"), ("z", "w", "y"), ("w", "y", "z"))
SIZES = {"y": 4, "z": 4, "w": 8}
AXIS_CODE = {"y": 0, "z": 1, "w": 2}
NEG = -1e30
BF = jnp.bfloat16
F32 = jnp.float32


def slot_tables():
    columns = np.zeros((SLOTS, 128), np.int32)
    rows = np.zeros((3, 16, SLOTS), np.int32)

    def keys_of(axes):
        shape = [SIZES[a] for a in axes] + [CAP]
        grids = np.meshgrid(*[np.arange(n) for n in shape], indexing="ij")
        return {name: grid.reshape(-1) for name, grid in zip(list(axes) + ["r"], grids)}

    def code(keys):
        return ((keys["y"] * 4 + keys["z"]) * 8 + keys["w"]) * CAP + keys["r"]

    def index(new, old):
        where = np.zeros(SLOTS, np.int32)
        where[code(old)] = np.arange(SLOTS)
        return where[code(new)]

    common = keys_of(("w", "z", "y"))
    for o, (a, b, c) in enumerate(ORDERS):
        first, second, third = keys_of((a, b, c)), keys_of((b, a, c)), keys_of((c, b, a))
        table = [
            first["y"], first["z"], first["w"] // 2, first["w"] % 2, first["r"],
            index(second, first), index(third, second), index(common, third),
        ]
        for i, entry in enumerate(table):
            columns[:, o * 8 + i] = entry
            rows[o, i] = entry
    return columns, rows


def kernel(
    q_ref, k_ref, v_ref, hid_ref, gain_ref, routes_ref, gates_ref, home_col_ref, home_row_ref,
    cols_ref, rows_ref, wg_hbm, wu_hbm, wd_hbm,
    ctx_ref, out_ref,
    send, recv, wgu, wd, perm, normed, placing, gating, hidden_acc, active,
    key_own, value_own, keys, values, qd, best, total, acc,
    send_sem, recv_sem, weight_sem, kv_send, kv_recv,
):
    y = lax.axis_index("ctx")
    flat = lax.axis_index("exp")
    z = lax.div(flat, 8)
    w = lax.rem(flat, 8)
    x = lax.div(w, 2)
    c = lax.rem(w, 2)

    def at(dy=0, dz=0, dx=0, dc=0):
        return (
            lax.rem(y + (dy + 4), 4),
            lax.rem(z + (dz + 4), 4) * 8 + lax.rem(x + (dx + 4), 4) * 2 + lax.rem(c + dc, 2),
        )

    barrier = pltpu.get_barrier_semaphore()
    partners = [at(dy=k) for k in (1, 2, 3)] + [at(dz=k) for k in (1, 2, 3)]
    partners += [at(dx=k // 2, dc=k % 2) for k in range(1, 8)]
    for partner in partners:
        pl.semaphore_signal(barrier, inc=1, device_id=partner, device_id_type=MESH)

    def gate_up_copies(j, slot):
        span = pl.ds(pl.multiple_of(j * CHUNK, CHUNK), CHUNK)
        return (
            pltpu.make_async_copy(wg_hbm.at[span], wgu.at[slot, 0], weight_sem.at[slot, 0]),
            pltpu.make_async_copy(wu_hbm.at[span], wgu.at[slot, 1], weight_sem.at[slot, 1]),
        )

    for slot in range(2):
        for copy in gate_up_copies(slot, slot):
            copy.start()
    down_copy = pltpu.make_async_copy(wd_hbm, wd, weight_sem.at[2, 0])
    down_copy.start()

    row64 = lax.broadcasted_iota(jnp.int32, (64, 64), 0)
    col64 = lax.broadcasted_iota(jnp.int32, (64, 64), 1)
    apart64 = (col64 == ((row64 & 31) * 2 + (row64 >> 5))).astype(BF)
    for source, own in ((k_ref, key_own), (v_ref, value_own)):
        parted = jnp.dot(apart64, source[...], preferred_element_type=F32).astype(BF)
        for head in range(2):
            for s in range(2):
                own[head, s] = parted[s * 32:(s + 1) * 32, head * 128:(head + 1) * 128]
    own_head = lax.div(z, 2)
    keys[:, 0, 0, 0, 0] = key_own[own_head]
    values[:, 0, 0, 0, 0] = value_own[own_head]

    pl.semaphore_wait(barrier, len(partners))

    def remote(source, target, step, kind, device):
        return pltpu.make_async_remote_copy(
            src_ref=source, dst_ref=target, send_sem=kv_send.at[step, kind],
            recv_sem=kv_recv.at[step, kind], device_id=device, device_id_type=MESH,
        )

    def kv_first():
        for k in (1, 2, 3):
            head = lax.div(lax.rem(z + k, 4), 2)
            remote(key_own.at[head], keys.at[:, 0, k, 0, 0], 0, 0, at(dz=k)).start()
            remote(value_own.at[head], values.at[:, 0, k, 0, 0], 0, 1, at(dz=k)).start()

    def kv_region(step):
        if step == 0:
            return keys.at[:, 0, pl.ds(1, 3), 0, 0], values.at[:, 0, pl.ds(1, 3), 0, 0]
        if step == 1:
            return keys.at[:, pl.ds(1, 3), :, 0, 0], values.at[:, 0, :, pl.ds(1, 3), 0]
        if step == 2:
            return keys.at[:, :, :, pl.ds(1, 3), 0], values.at[:, pl.ds(1, 3), :, :, 0]
        return keys.at[:, :, :, :, 1], values.at[:, :, :, :, 1]

    def kv_wait(step, sent):
        for kind, region in enumerate(kv_region(step)):
            copy = remote(region, region, step, kind, at(dc=1))
            if sent:
                copy.wait_send()
            else:
                copy.wait_recv()

    def kv_second():
        for k in (2, 1, 3):
            remote(keys.at[:, 0, :, 0, 0], keys.at[:, k, :, 0, 0], 1, 0, at(dy=k)).start()
            remote(values.at[:, 0, :, 0, 0], values.at[:, 0, :, k, 0], 1, 1, at(dx=k)).start()

    def kv_third():
        for k in (2, 1, 3):
            remote(keys.at[:, :, :, 0, 0], keys.at[:, :, :, k, 0], 2, 0, at(dx=k)).start()
            remote(values.at[:, 0, :, :, 0], values.at[:, k, :, :, 0], 2, 1, at(dy=k)).start()

    def kv_fourth():
        remote(keys.at[:, :, :, :, 0], keys.at[:, :, :, :, 1], 3, 0, at(dc=1)).start()
        remote(values.at[:, :, :, :, 0], values.at[:, :, :, :, 1], 3, 1, at(dc=1)).start()

    kv_first()

    tokens = hid_ref[...].astype(F32)
    scale = lax.rsqrt(jnp.mean(tokens * tokens, axis=-1, keepdims=True) + 1e-06)
    for j in range(CHUNKS):
        span = slice(j * CHUNK, (j + 1) * CHUNK)
        part = hid_ref[:, span].astype(F32)
        normed[j] = (part * scale * gain_ref[:, span]).astype(BF)

    expert_lane = lax.broadcasted_iota(jnp.int32, (TOKENS, 128), 1)
    picked = jnp.zeros((TOKENS, 128), F32)
    gate_of = jnp.zeros((TOKENS, 128), F32)
    for k in range(TOPK):
        hit = routes_ref[:, k:k + 1] == expert_lane
        picked = picked + jnp.where(hit, 1.0, 0.0)
        gate_of = gate_of + jnp.where(hit, gates_ref[:, k:k + 1], 0.0)
    earlier = (col64 < row64).astype(BF)
    before = jnp.dot(earlier, picked.astype(BF), preferred_element_type=F32)
    gate_high = gate_of.astype(BF)
    gate_low = (gate_of - gate_high.astype(F32)).astype(BF)
    facts = jnp.concatenate([picked.astype(BF), before.astype(BF), gate_high, gate_low], axis=0)
    for o in range(3):
        def target(field):
            return (
                ((y + field(0)) & 3) * 32 + ((z + field(1)) & 3) * 8
                + ((x + field(2)) & 3) * 2 + ((c + field(3)) & 1)
            )

        dest_col = target(lambda i: cols_ref[:, o * 8 + i:o * 8 + i + 1])
        dest_row = target(lambda i: rows_ref[o, i:i + 1, :])
        hosts_t = (dest_col == home_row_ref[...]).astype(BF)
        hosts = (dest_row == home_col_ref[...]).astype(BF)
        slot_facts_t = lax.dot_general(
            hosts_t, facts[:128], (((1,), (1,)), ((), ())), preferred_element_type=F32
        )
        rank_col = cols_ref[:, o * 8 + 4:o * 8 + 5].astype(F32)
        placing[o] = (
            slot_facts_t[:, :64] * jnp.where(slot_facts_t[:, 64:] == rank_col, 1.0, 0.0)
        ).astype(BF)
        slot_facts = jnp.dot(facts, hosts, preferred_element_type=F32)
        rank_row = rows_ref[o, 4:5, :].astype(F32)
        kept = slot_facts[:64] * jnp.where(slot_facts[64:128] == rank_row, 1.0, 0.0)
        gating[o] = (slot_facts[128:] * jnp.concatenate([kept, kept], axis=0)).astype(BF)

    lane = lax.broadcasted_iota(jnp.int32, (SLOTS, SLOTS), 1)
    sublane = lax.broadcasted_iota(jnp.int32, (SLOTS, SLOTS), 0)
    for o in range(3):
        for i in range(3):
            perm[o * 5 + i] = jnp.where(
                cols_ref[:, o * 8 + 5 + i:o * 8 + 6 + i] == lane, 1.0, 0.0
            ).astype(BF)
        for i in range(2):
            perm[o * 5 + 3 + i] = jnp.where(
                rows_ref[o, 5 + i:6 + i, :] == sublane, 1.0, 0.0
            ).astype(BF)

    def axis_of(o, hop):
        return lax.rem(o + hop, 3)

    def by_axis(axis, four, eight):
        pl.when(axis == 0)(lambda: four(0))
        pl.when(axis == 1)(lambda: four(1))
        pl.when(axis == 2)(eight)

    def piece(stage, j, first, count, device):
        return pltpu.make_async_remote_copy(
            src_ref=send.at[stage % 3, j, pl.ds(first, count)],
            dst_ref=recv.at[stage, j, pl.ds(first, count)],
            send_sem=send_sem.at[stage, j], recv_sem=recv_sem.at[stage, j],
            device_id=device, device_id_type=MESH,
        )

    def start_hop(stage, j, axis):
        sign = 1 if stage < 3 else -1

        def four(which):
            for k in (2, 1, 3):
                device = at(dy=sign * k) if which == 0 else at(dz=sign * k)
                piece(stage, j, 96 * k, 96, device).start()
            recv[stage, j, 0:96] = send[stage % 3, j, 0:96]

        def eight():
            for k in (4, 5, 2, 6, 3, 7, 1):
                piece(stage, j, 48 * k, 48, at(dx=sign * (k // 2), dc=k % 2)).start()
            recv[stage, j, 0:48] = send[stage % 3, j, 0:48]

        by_axis(axis, four, eight)

    def wait_hop(stage, j, axis):
        here = at(dc=1)
        by_axis(
            axis,
            lambda which: piece(stage, j, 96, 288, here).wait_recv(),
            lambda: piece(stage, j, 48, 336, here).wait_recv(),
        )

    def wait_sent(stage, j, axis):
        here = at(dc=1)
        by_axis(
            axis,
            lambda which: piece(stage, j, 96, 288, here).wait_send(),
            lambda: piece(stage, j, 48, 336, here).wait_send(),
        )

    def reorder(stage, j, matrix):
        for half in range(2):
            span = pl.ds(half * (CHUNK // 2), CHUNK // 2)
            send[(stage + 1) % 3, j, :, span] = jnp.dot(
                perm[matrix], recv[stage, j, :, span], preferred_element_type=F32
            ).astype(BF)

    def loop(step):
        def one(j, carry):
            step(j, lax.rem(j, 3))
            return carry

        lax.fori_loop(0, CHUNKS, one, 0)

    kv_wait(0, False)
    kv_second()

    def place_step(j, o):
        send[0, j] = jnp.dot(placing[o], normed[j], preferred_element_type=F32).astype(BF)
        start_hop(0, j, axis_of(o, 0))

    loop(place_step)

    row256 = lax.broadcasted_iota(jnp.int32, (256, 256), 0)
    col256 = lax.broadcasted_iota(jnp.int32, (256, 256), 1)
    apart256 = (col256 == ((row256 & 127) * 2 + (row256 >> 7))).astype(BF)
    for b in range(8):
        parted = jnp.dot(
            apart256, q_ref[b * 256:(b + 1) * 256], preferred_element_type=F32
        ).astype(BF)
        for s in range(2):
            qd[s, b * 128:(b + 1) * 128] = parted[s * 128:(s + 1) * 128]
    best[...] = jnp.full_like(best, NEG)
    total[...] = jnp.zeros_like(total)
    acc[...] = jnp.zeros_like(acc)

    kv_wait(1, False)
    kv_third()

    def second_step(j, o):
        wait_hop(0, j, axis_of(o, 0))
        reorder(0, j, o * 5)
        start_hop(1, j, axis_of(o, 1))

    loop(second_step)

    kv_wait(2, False)
    kv_fourth()

    def third_step(j, o):
        wait_hop(1, j, axis_of(o, 1))
        reorder(1, j, o * 5 + 1)
        start_hop(2, j, axis_of(o, 2))

    loop(third_step)

    hidden_acc[...] = jnp.zeros_like(hidden_acc)

    def project_step(j, o):
        wait_hop(2, j, axis_of(o, 2))
        slot = lax.rem(j, 2)
        for copy in gate_up_copies(j, slot):
            copy.wait()
        rows_in = jnp.dot(perm[o * 5 + 2], recv[2, j], preferred_element_type=F32).astype(BF)
        for which in range(2):
            for part in range(2):
                span = pl.ds(part * 384, 384)
                hidden_acc[which, :, span] += jnp.dot(
                    rows_in, wgu[slot, which, :, span], preferred_element_type=F32
                )

        @pl.when(j + 2 < CHUNKS)
        def _():
            for copy in gate_up_copies(j + 2, slot):
                copy.start()

    loop(project_step)

    gate_proj = hidden_acc[0]
    rows_mid = (gate_proj / (1.0 + jnp.exp(-gate_proj)) * hidden_acc[1]).astype(BF)
    for o in range(3):
        back = jnp.where(rows_ref[o, 7:8, :] == sublane, 1.0, 0.0).astype(BF)
        active[o] = jnp.dot(back, rows_mid, preferred_element_type=F32).astype(BF)
    down_copy.wait()

    def produce_step(j, o):
        wait_sent(0, j, axis_of(o, 0))
        span = pl.ds(pl.multiple_of(j * CHUNK, CHUNK), CHUNK)
        send[0, j] = jnp.dot(active[o], wd[:, span], preferred_element_type=F32).astype(BF)
        start_hop(3, j, axis_of(o, 2))

    loop(produce_step)

    kv_wait(3, False)
    lane_key = lax.broadcasted_iota(jnp.int32, (1, BLOCK), 1)
    key_pos = (
        ((z + 4 - (lane_key >> 8)) & 3) * 256
        + ((x + 4 - ((lane_key >> 6) & 3)) & 3) * 64
        + ((c + (lane_key >> 5)) & 1) * 32
        + (lane_key & 31)
    )
    factor = HEAD_WIDTH ** (-0.5) * 1.4426950408889634

    def attend(t):
        behind = lax.div(t, 4)
        s = lax.rem(lax.div(t, 2), 2)
        half = lax.rem(t, 2)

        @pl.when(behind <= y)
        def _():
            block_keys = keys[s, behind].reshape(BLOCK, HEAD_WIDTH)
            block_values = values[s, behind].reshape(BLOCK, HEAD_WIDTH)
            for q in range(2):
                first = pl.multiple_of(half * 512 + q * 256, 256)
                span = pl.ds(first, 256)
                scores = lax.dot_general(
                    qd[s, span], block_keys, (((1,), (1,)), ((), ())),
                    preferred_element_type=F32,
                ) * factor
                query_pos = lax.broadcasted_iota(jnp.int32, (256, 1), 0) + (
                    first + behind * BLOCK
                )
                scores = jnp.where(key_pos <= query_pos, scores, NEG)
                best_old = best[s, span]
                best_new = jnp.maximum(best_old, jnp.max(scores, axis=-1, keepdims=True))
                weights = jnp.exp2(scores - best_new[:, :1])
                shrink = jnp.exp2(best_old - best_new)
                best[s, span] = best_new
                total[s, span] = total[s, span] * shrink + jnp.sum(
                    weights, axis=-1, keepdims=True
                )
                acc[s, span] = acc[s, span] * shrink + jnp.dot(
                    weights.astype(BF), block_values, preferred_element_type=F32
                )

    def return_second_step(j, o):
        wait_hop(3, j, axis_of(o, 2))
        wait_sent(1, j, axis_of(o, 1))
        reorder(3, j, o * 5 + 4)
        start_hop(4, j, axis_of(o, 1))
        attend(j)

    loop(return_second_step)

    def return_third_step(j, o):
        wait_hop(4, j, axis_of(o, 1))
        wait_sent(2, j, axis_of(o, 2))
        reorder(4, j, o * 5 + 3)
        start_hop(5, j, axis_of(o, 0))
        attend(j + 8)

    loop(return_third_step)

    together = (col256 == ((row256 & 1) * 128 + (row256 >> 1))).astype(BF)
    for b in range(8):
        span = slice(b * 128, (b + 1) * 128)
        both = jnp.concatenate(
            [(acc[s, span] / total[s, span]).astype(BF) for s in range(2)], axis=0
        )
        ctx_ref[b * 256:(b + 1) * 256] = jnp.dot(
            together, both, preferred_element_type=F32
        ).astype(BF)

    def combine_step(j, o):
        wait_hop(5, j, axis_of(o, 0))
        span = pl.ds(pl.multiple_of(j * CHUNK, CHUNK), CHUNK)
        mixed = jnp.dot(gating[o], recv[5, j], preferred_element_type=F32)
        out_ref[:, span] = (
            hid_ref[:, span].astype(F32) + mixed[:64] + mixed[64:]
        ).astype(BF)

    loop(combine_step)

    def drain_step(j, o):
        wait_sent(3, j, axis_of(o, 2))
        wait_sent(4, j, axis_of(o, 1))
        wait_sent(5, j, axis_of(o, 0))

    loop(drain_step)
    for step in range(4):
        kv_wait(step, True)


def body(
    queries, key_rows, values, hidden, norm_gain, routes, route_gates, expert_home,
    w_gate, w_up, w_down,
):
    columns, rows = slot_tables()
    vmem = pl.BlockSpec(memory_space=pltpu.VMEM)
    hbm = pl.BlockSpec(memory_space=pl.ANY)
    block = (CHUNKS, SLOTS, CHUNK)
    context, layer_out = pl.pallas_call(
        kernel,
        out_shape=(
            jax.ShapeDtypeStruct((2 * BLOCK, HEAD_WIDTH), BF),
            jax.ShapeDtypeStruct((TOKENS, WIDTH), BF),
        ),
        in_specs=[vmem] * 11 + [hbm] * 3,
        out_specs=(vmem, vmem),
        scratch_shapes=[
            pltpu.VMEM((3,) + block, BF),
            pltpu.VMEM((6,) + block, BF),
            pltpu.VMEM((2, 2, CHUNK, FF), BF),
            pltpu.VMEM((FF, WIDTH), BF),
            pltpu.VMEM((15, SLOTS, SLOTS), BF),
            pltpu.VMEM((CHUNKS, TOKENS, CHUNK), BF),
            pltpu.VMEM((3, SLOTS, TOKENS), BF),
            pltpu.VMEM((3, 2 * TOKENS, SLOTS), BF),
            pltpu.VMEM((2, SLOTS, FF), F32),
            pltpu.VMEM((3, SLOTS, FF), BF),
            pltpu.VMEM((2, 2, 32, HEAD_WIDTH), BF),
            pltpu.VMEM((2, 2, 32, HEAD_WIDTH), BF),
            pltpu.VMEM((2, 4, 4, 4, 2, 32, HEAD_WIDTH), BF),
            pltpu.VMEM((2, 4, 4, 4, 2, 32, HEAD_WIDTH), BF),
            pltpu.VMEM((2, BLOCK, HEAD_WIDTH), BF),
            pltpu.VMEM((2, BLOCK, HEAD_WIDTH), F32),
            pltpu.VMEM((2, BLOCK, HEAD_WIDTH), F32),
            pltpu.VMEM((2, BLOCK, HEAD_WIDTH), F32),
            pltpu.SemaphoreType.DMA((6, CHUNKS)),
            pltpu.SemaphoreType.DMA((6, CHUNKS)),
            pltpu.SemaphoreType.DMA((3, 2)),
            pltpu.SemaphoreType.DMA((4, 2)),
            pltpu.SemaphoreType.DMA((4, 2)),
        ],
        compiler_params=pltpu.CompilerParams(
            collective_id=0, has_side_effects=True, vmem_limit_bytes=62 * 2**20
        ),
    )(
        queries.reshape(2 * BLOCK, HEAD_WIDTH),
        key_rows.reshape(TOKENS, 2 * HEAD_WIDTH),
        values.reshape(TOKENS, 2 * HEAD_WIDTH),
        hidden.reshape(TOKENS, WIDTH),
        norm_gain.reshape(1, WIDTH),
        routes.reshape(TOKENS, TOPK),
        route_gates.reshape(TOKENS, TOPK),
        expert_home.reshape(128, 1),
        expert_home.reshape(1, 128),
        jnp.asarray(columns),
        jnp.asarray(rows),
        w_gate[0],
        w_up[0],
        w_down[0],
    )
    return context.reshape(queries.shape), layer_out.reshape(hidden.shape)


def solution(mesh):
    both = P(("ctx", "exp"), None, None)
    in_specs = (P("ctx", None, "exp"), both, both, both, P(), both, both, P(), both, both, both)
    out_specs = (P("ctx", None, "exp"), both)
    return jax.shard_map(body, mesh=mesh, in_specs=in_specs, out_specs=out_specs, check_vma=False)
```

time: 327 us -> 123 us (0.38)
  the two profiles are of different devices: /device:TPU:60 before, /device:TPU:25 now
where the time goes in v1:
time: 123 us; the launch traced here: 122 us
  Pallas kernels  108 us (88%)
  local copies, waits for them, and re-layouts  13.3 us (11%)
    pallas_call x1, Pallas kernels, body(): pl.pallas_call(kernel, out_shape=(jax.ShapeDtypeStruct((2 * BLOCK, HEAD_W...  108 us
    unnamed x3, local copies, waits for them, and re-layouts  4.98 us

profile of v1, /device:TPU:25, one launch (start us, length us, event | category | flops | bytes accessed | tf_op | source)
XLA Modules:
  0.0 121.9 jit_solution(3685730491295030712)
XLA Ops:
  0.6 1.4 %reshape.38.k_ref = bf16[64,256]{1,0:T(8,128)(2,1)} reshape(bf16[32,2,256]{2,1,0:T(2,128)(2,1)} %param.14) | data formatting | bytes 65536 | tf_op jit(solution)/shard_map/reshape | solution.py:488
  2.0 1.4 %reshape.39.v_ref = bf16[64,256]{1,0:T(8,128)(2,1)} reshape(bf16[32,2,256]{2,1,0:T(2,128)(2,1)} %param.15) | data formatting | bytes 65536 | tf_op jit(solution)/shard_map/reshape | solution.py:489
  3.4 1.4 %copy.15 = s32[32,2,8]{2,1,0:T(2,128)} copy(s32[32,2,8]{0,2,1:T(8,128)} %param.18) | data formatting | bytes 4096 | tf_op args[5]
  4.8 1.4 %copy.16 = f32[32,2,8]{2,1,0:T(2,128)} copy(f32[32,2,8]{0,2,1:T(8,128)} %param.19) | data formatting | bytes 4096 | tf_op args[6]
  6.2 1.4 %copy.17.home_col_ref = s32[128,1]{1,0:T(8,128)} copy(s32[128,1]{0,1:T(1,128)} %bitcast.18) | data formatting | bytes 1024 | tf_op jit(solution)/shard_map/reshape | solution.py:494
  7.6 2.0 %reshape.40.hid_ref = bf16[64,4096]{1,0:T(8,128)(2,1)} reshape(bf16[32,2,4096]{2,1,0:T(2,128)(2,1)} %param.16) | data formatting | bytes 1048576 | tf_op jit(solution)/shard_map/reshape | solution.py:490
  9.6 107.9 %shard_map.140 = (bf16[2048,128]{1,0:T(8,128)(2,1)}, bf16[64,4096]{1,0:T(8,128)(2,1)}) custom-call(bf16[2048,128]{1,0:T(8,128)(2,1)} %bitcast.13, bf16[64,256]{1,0:T(8,128)(2,1)} %reshape.38.k_ref, bf16[64,256]{1,0:T(8,128)(2,1)} %reshape.39.v_ref, bf16[64,4096]{1,0:T(8,128)(2,1)} %reshape.40.hid_ref, f32[1,4096]{1,0:T(1,128)} %bitcast.17, ...), custom_call_target="tpu_custom_call" | custom-call | tf_op jit(solution)/shard_map/pallas_call | solution.py:450
  117.6 2.2 %reshape.47 = bf16[32,2,4096]{2,1,0:T(2,128)(2,1)} reshape(bf16[64,4096]{1,0:T(8,128)(2,1)} %get-tuple-element.5) | data formatting | bytes 1048576 | tf_op jit(solution)/shard_map/reshape | solution.py:502
  119.7 2.2 %copy.19 = bf16[1024,2,128]{2,1,0:T(2,128)(2,1)} copy(bf16[1024,2,128]{2,1,0:T(2,128)(2,1)} %bitcast.14) | data formatting | bytes 1048576

commit v2 on v1

v2 whole, which is shorter than its diff:
```python
import jax
import jax.numpy as jnp
import numpy as np
from jax import lax
from jax.experimental import pallas as pl
from jax.experimental.pallas import tpu as pltpu
from jax.sharding import PartitionSpec as P

MESH = pl.DeviceIdType.MESH
HEAD_WIDTH = 128
TOPK = 8
WIDTH = 4096
FF = 768
CAP = 3
TOKENS = 64
SLOTS = 384
CHUNKS = 8
CHUNK = WIDTH // CHUNKS
BLOCK = 1024
ORDERS = (("y", "z", "x"), ("z", "x", "y"), ("x", "y", "z"))
NEG = -1e30
BF = jnp.bfloat16
F32 = jnp.float32


def slot_tables():
    grids = np.indices((4, 4, 8, CAP)).reshape(4, SLOTS)

    def index(new, old, sizes):
        where = np.zeros(SLOTS, np.int32)
        where[np.ravel_multi_index(old, sizes)] = np.arange(SLOTS)
        return where[np.ravel_multi_index(new, sizes)]

    by_start = list(grids)
    by_middle = np.indices((4, 4, 8, CAP)).reshape(4, SLOTS)[[1, 0, 2, 3]]
    by_end = np.indices((8, 4, 4, CAP)).reshape(4, SLOTS)[[2, 1, 0, 3]]
    sizes = (4, 4, 8, CAP)
    columns = np.zeros((SLOTS, 128), np.int32)
    rows = np.zeros((8, SLOTS), np.int32)
    columns[:, 0] = index(by_middle, by_start, sizes)
    columns[:, 1] = index(by_end, by_middle, sizes)
    rows[0] = columns[:, 1]

    def offsets(keys, axes):
        found = dict(zip(axes, (keys[0], keys[1], keys[2] // 2)))
        return [found["y"], found["z"], found["x"], keys[2] % 2, keys[3]]

    common = offsets(by_end, ORDERS[0])
    for o, axes in enumerate(ORDERS):
        for i, entry in enumerate(offsets(by_start, axes)):
            columns[:, 8 + o * 8 + i] = entry
        rows[1 + o] = index(common, offsets(by_end, axes), (4, 4, 4, 2, CAP))
        columns[:, 2 + o] = rows[1 + o]
    return columns, rows


def kernel(
    q_ref, k_ref, v_ref, hid_ref, gain_ref, routes_ref, gates_ref, home_ref,
    cols_ref, rows_ref, wg_hbm, wu_hbm, wd_hbm,
    ctx_ref, out_ref,
    send, recv, recv_first, recv_last, wgu, wd, perm, normed, gates_own, gates_all, placing,
    gating, hidden_acc, rows_in, active,
    key_own, value_own, keys, values, qd, best, total, acc,
    send_sem, recv_sem, gate_send, gate_recv, weight_sem, kv_send, kv_recv,
):
    y = lax.axis_index("ctx")
    flat = lax.axis_index("exp")
    z = lax.div(flat, 8)
    w = lax.rem(flat, 8)
    x = lax.div(w, 2)
    c = lax.rem(w, 2)

    def at(dy=0, dz=0, dx=0, dc=0):
        return (
            lax.rem(y + (dy + 4), 4),
            lax.rem(z + (dz + 4), 4) * 8 + lax.rem(x + (dx + 4), 4) * 2 + lax.rem(c + dc, 2),
        )

    barrier = pltpu.get_barrier_semaphore()
    partners = [at(dc=1)]
    for axis in ("dy", "dz", "dx"):
        partners += [at(**{axis: k, "dc": n}) for k in (1, 2, 3) for n in (0, 1)]
    for partner in partners:
        pl.semaphore_signal(barrier, inc=1, device_id=partner, device_id_type=MESH)

    def gate_up_copies(j, slot):
        span = pl.ds(pl.multiple_of(j * CHUNK, CHUNK), CHUNK)
        return (
            pltpu.make_async_copy(wg_hbm.at[span], wgu.at[slot, 0], weight_sem.at[slot, 0]),
            pltpu.make_async_copy(wu_hbm.at[span], wgu.at[slot, 1], weight_sem.at[slot, 1]),
        )

    for slot in range(2):
        for copy in gate_up_copies(slot, slot):
            copy.start()
    down_copy = pltpu.make_async_copy(wd_hbm, wd, weight_sem.at[2, 0])
    down_copy.start()

    row256 = lax.broadcasted_iota(jnp.int32, (256, 256), 0)
    col256 = lax.broadcasted_iota(jnp.int32, (256, 256), 1)
    apart_tiles = (
        col256 == (row256 & 3) * 64 + (row256 >> 3) * 2 + ((row256 >> 2) & 1)
    ).astype(BF)
    for b in range(8):
        parted = jnp.dot(
            apart_tiles, hid_ref[b * 256:(b + 1) * 256], preferred_element_type=F32
        )
        for tile in range(32):
            out_ref[b * 8:(b + 1) * 8, tile * 128:(tile + 1) * 128] = (
                parted[tile * 8:(tile + 1) * 8]
            )

    tokens = out_ref[...]
    scale = lax.rsqrt(jnp.mean(tokens * tokens, axis=-1, keepdims=True) + 1e-06)
    for j in range(CHUNKS):
        span = slice(j * CHUNK, (j + 1) * CHUNK)
        normed[j] = (out_ref[:, span] * scale * gain_ref[:, span]).astype(BF)

    row128 = lax.broadcasted_iota(jnp.int32, (128, 128), 0)
    col128 = lax.broadcasted_iota(jnp.int32, (128, 128), 1)
    apart128 = (
        col128 == (row128 & 31) * 4 + (row128 >> 6) * 2 + ((row128 >> 5) & 1)
    ).astype(BF)
    for source, own in ((k_ref, key_own), (v_ref, value_own)):
        parted = jnp.dot(apart128, source[...], preferred_element_type=F32).astype(BF)
        for head in range(2):
            for s in range(2):
                first = head * 64 + s * 32
                own[head, s] = parted[first:first + 32]
    own_head = lax.div(z, 2)
    keys[:, 0, 0, 0, 0] = key_own[own_head]
    values[:, 0, 0, 0, 0] = value_own[own_head]

    def remote(source, target, step, kind, n, device):
        return pltpu.make_async_remote_copy(
            src_ref=source, dst_ref=target, send_sem=kv_send.at[step, kind, n],
            recv_sem=kv_recv.at[step, kind, n], device_id=device, device_id_type=MESH,
        )

    def kv_first():
        for k in (1, 2, 3):
            head = lax.div(lax.rem(z + k, 4), 2)
            remote(key_own.at[head], keys.at[:, 0, k, 0, 0], 0, 0, 0, at(dz=k)).start()
            remote(value_own.at[head], values.at[:, 0, k, 0, 0], 0, 1, 0, at(dz=k)).start()

    def kv_second():
        for k in (2, 1, 3):
            @pl.when(y + k < 4)
            def _():
                remote(keys.at[:, 0, :, 0, 0], keys.at[:, k, :, 0, 0], 1, 0, k, at(dy=k)).start()

            remote(values.at[:, 0, :, 0, 0], values.at[:, 0, :, k, 0], 1, 1, 0, at(dx=k)).start()

    def kv_third():
        for k in (2, 1, 3):
            @pl.when(y + k < 4)
            def _():
                remote(values.at[:, 0, :, :, 0], values.at[:, k, :, :, 0], 2, 1, k, at(dy=k)).start()

        for n in range(4):
            @pl.when(n <= y)
            def _():
                for k in (2, 1, 3):
                    remote(keys.at[:, n, :, 0, 0], keys.at[:, n, :, k, 0], 2, 0, n, at(dx=k)).start()

    def kv_fourth():
        for n in range(4):
            @pl.when(n <= y)
            def _():
                remote(keys.at[:, n, :, :, 0], keys.at[:, n, :, :, 1], 3, 0, n, at(dc=1)).start()
                remote(values.at[:, n, :, :, 0], values.at[:, n, :, :, 1], 3, 1, n, at(dc=1)).start()

    def kv_wait(step, sent):
        def wait(region, kind, n):
            copy = remote(region, region, step, kind, n, at(dc=1))
            if sent:
                copy.wait_send()
            else:
                copy.wait_recv()

        if step == 0:
            wait(keys.at[:, 0, pl.ds(1, 3), 0, 0], 0, 0)
            wait(values.at[:, 0, pl.ds(1, 3), 0, 0], 1, 0)
        if step == 1:
            wait(values.at[:, 0, :, pl.ds(1, 3), 0], 1, 0)
        for n in range(4):
            if step in (1, 2) and n > 0:
                @pl.when(y + n < 4 if sent else n <= y)
                def _():
                    if step == 1:
                        wait(keys.at[:, n, :, 0, 0], 0, n)
                    else:
                        wait(values.at[:, n, :, :, 0], 1, n)

            if step in (2, 3):
                @pl.when(n <= y)
                def _():
                    if step == 2:
                        wait(keys.at[:, n, :, pl.ds(1, 3), 0], 0, n)
                    else:
                        wait(keys.at[:, n, :, :, 1], 0, n)
                        wait(values.at[:, n, :, :, 1], 1, n)

    def sources(stage, j):
        if stage == 0:
            return None, recv_first.at[j]
        if stage == 5:
            return send.at[0, j], recv_last.at[j]
        return send.at[(stage + 1) % 2, j], recv.at[stage - 1, j]

    group_rows = (64, 96, 48, 48, 96, 64)

    def piece(stage, j, group, groups, device):
        source, target = sources(stage, j)
        span = pl.ds(group * group_rows[stage], groups * group_rows[stage])
        if stage == 0:
            source = normed.at[j] if groups == 1 else target.at[span]
        else:
            source = source.at[span]
        return pltpu.make_async_remote_copy(
            src_ref=source, dst_ref=target.at[span],
            send_sem=send_sem.at[stage, j], recv_sem=recv_sem.at[stage, j],
            device_id=device, device_id_type=MESH,
        )

    def along(o, hop, act):
        for n, axes in enumerate(ORDERS):
            pl.when(o == n)(lambda axis="d" + axes[hop]: act(axis))

    def start_hop(stage, j, o):
        hop = stage if stage < 3 else 5 - stage
        sign = 1 if stage < 3 else -1

        def start(axis):
            if hop == 2:
                for k in (4, 5, 2, 6, 3, 7, 1):
                    device = at(**{axis: sign * (k // 2), "dc": k % 2})
                    piece(stage, j, k, 1, device).start()
            else:
                for k in (2, 1, 3):
                    piece(stage, j, k, 1, at(**{axis: sign * k})).start()

        along(o, hop, start)
        rows = group_rows[stage]
        source, target = sources(stage, j)
        if stage == 0:
            target[0:rows] = normed[j]
        else:
            target[0:rows] = source[0:rows]

    def wait_hop(stage, j):
        piece(stage, j, 1, 7 if stage in (2, 3) else 3, at(dc=1)).wait_recv()

    def wait_sent(stage, j):
        piece(stage, j, 1, 7 if stage in (2, 3) else 3, at(dc=1)).wait_send()

    def loop(step, first=0, last=CHUNKS):
        def one(j, carry):
            step(j)
            return carry

        lax.fori_loop(first, last, one, 0)

    def order(j):
        return lax.rem(j, 3)

    pl.semaphore_wait(barrier, len(partners))


    kv_first()
    loop(lambda j: start_hop(0, j, order(j)), 0, 4)

    expert_row = lax.broadcasted_iota(jnp.int32, (128, 32), 0)
    picked_parts, gate_parts = [], []
    for s in range(2):
        picked = jnp.zeros((128, 32), F32)
        gate_of = jnp.zeros((128, 32), F32)
        for k in range(TOPK):
            n = s * TOPK + k
            hit = routes_ref[n:n + 1, :] == expert_row
            picked = picked + jnp.where(hit, 1.0, 0.0)
            gate_of = gate_of + jnp.where(hit, gates_ref[n:n + 1, :], 0.0)
        picked_parts.append(picked)
        gate_parts.append(gate_of)
    picked = jnp.concatenate(picked_parts, axis=1)
    gate_of = jnp.concatenate(gate_parts, axis=1)
    row64 = lax.broadcasted_iota(jnp.int32, (64, 64), 0)
    col64 = lax.broadcasted_iota(jnp.int32, (64, 64), 1)
    position = (col64 >> 3) * 4 + (col64 & 3)
    sequence = (col64 >> 2) & 1
    in_order = (row64 == sequence * 32 + position).astype(BF)
    earlier = ((row64 & 31) * 2 + (row64 >> 5) < position * 2 + sequence).astype(BF)
    gate_high = gate_of.astype(BF)
    gate_low = (gate_of - gate_high.astype(F32)).astype(BF)
    facts = [
        jnp.dot(part, matrix, preferred_element_type=F32).astype(BF)
        for part, matrix in (
            (picked.astype(BF), in_order), (picked.astype(BF), earlier),
            (gate_high, in_order), (gate_low, in_order),
        )
    ]
    def gate_copy(o, group, groups, device):
        span = pl.ds(96 * group, 96 * groups)
        return pltpu.make_async_remote_copy(
            src_ref=gates_own.at[o, span], dst_ref=gates_all.at[o, span],
            send_sem=gate_send.at[o], recv_sem=gate_recv.at[o],
            device_id=device, device_id_type=MESH,
        )

    for o in range(3):
        def target(field):
            return (
                ((y + field(0)) & 3) * 32 + ((z + field(1)) & 3) * 8
                + ((x + field(2)) & 3) * 2 + ((c + field(3)) & 1)
            )

        dest = target(lambda i: cols_ref[:, 8 + o * 8 + i:9 + o * 8 + i])
        hosts = (dest == home_ref[...]).astype(BF)
        named, rank, high, low = [
            jnp.dot(hosts, fact, preferred_element_type=F32) for fact in facts
        ]
        kept = named * jnp.where(
            rank == cols_ref[:, 12 + o * 8:13 + o * 8].astype(F32), 1.0, 0.0
        )
        gates_own[o] = jnp.concatenate([high * kept, low * kept], axis=1).astype(BF)
        gates_all[o, 0:96] = gates_own[o, 0:96]
        for k in (1, 2, 3):
            gate_copy(o, k, 1, at(**{"d" + ORDERS[o][0]: k})).start()

    loop(lambda j: start_hop(0, j, order(j)), 4, 8)
    kv_wait(0, False)
    kv_second()

    lane = lax.broadcasted_iota(jnp.int32, (SLOTS, SLOTS), 1)
    sublane = lax.broadcasted_iota(jnp.int32, (SLOTS, SLOTS), 0)
    for i in (0, 1, 3, 4):
        perm[i] = jnp.where(cols_ref[:, i:i + 1] == lane, 1.0, 0.0).astype(BF)
    perm[2] = jnp.where(rows_ref[0:1, :] == sublane, 1.0, 0.0).astype(BF)

    def reorder(stage, j, matrix):
        for half in range(2):
            span = pl.ds(half * (CHUNK // 2), CHUNK // 2)
            send[stage % 2, j, :, span] = jnp.dot(
                perm[matrix], recv[stage - 1, j, :, span], preferred_element_type=F32
            ).astype(BF)

    own_group = (
        lax.broadcasted_iota(jnp.int32, (SLOTS, 256), 1) >> 6
        == lax.div(lax.broadcasted_iota(jnp.int32, (SLOTS, 256), 0), 96)
    )
    for o in range(3):
        gate_copy(o, 1, 3, at(dc=1)).wait_recv()
        high = gates_all[o, :, 0:64].astype(F32)
        filled = jnp.where(
            jnp.logical_and(own_group, jnp.concatenate([high] * 4, axis=1) != 0.0), 1.0, 0.0
        ).astype(BF)
        placing[o] = jnp.dot(perm[0], filled, preferred_element_type=F32).astype(BF)

    def build_gating():
        for o in range(3):
            for n in range(2):
                part = gates_all[o, :, n * 64:(n + 1) * 64].astype(F32)
                spread = jnp.where(own_group, jnp.concatenate([part] * 4, axis=1), 0.0)
                gating[o, n * 256:(n + 1) * 256] = jnp.transpose(
                    jnp.dot(perm[0], spread.astype(BF), preferred_element_type=F32)
                ).astype(BF)

    def second_step(j):
        o = order(j)
        wait_hop(0, j)
        for half in range(2):
            span = pl.ds(half * (CHUNK // 2), CHUNK // 2)
            send[0, j, :, span] = jnp.dot(
                placing[o], recv_first[j, :, span], preferred_element_type=F32
            ).astype(BF)
        start_hop(1, j, o)

    def third_step(j):
        o = order(j)
        wait_hop(1, j)
        reorder(1, j, 1)
        start_hop(2, j, o)

    def project_step(j):
        o = order(j)
        wait_hop(2, j)
        slot = lax.rem(j, 2)
        for copy in gate_up_copies(j, slot):
            copy.wait()

        @pl.when(o == 0)
        def _():
            rows_in[...] = recv[1, j]

        @pl.when(o > 0)
        def _():
            rows_in[...] = jnp.dot(
                perm[o + 2], recv[1, j], preferred_element_type=F32
            ).astype(BF)

        for which in range(2):
            for part in range(2):
                span = pl.ds(part * 384, 384)
                hidden_acc[which, :, span] += jnp.dot(
                    rows_in[...], wgu[slot, which, :, span], preferred_element_type=F32
                )

        @pl.when(j + 2 < CHUNKS)
        def _():
            for copy in gate_up_copies(j + 2, slot):
                copy.start()

    loop(second_step, 0, 4)

    apart256 = (col256 == ((row256 & 127) * 2 + (row256 >> 7))).astype(BF)
    for b in range(8):
        parted = jnp.dot(
            apart256, q_ref[b * 256:(b + 1) * 256], preferred_element_type=F32
        ).astype(BF)
        for s in range(2):
            qd[s, b * 128:(b + 1) * 128] = parted[s * 128:(s + 1) * 128]
    best[...] = jnp.full_like(best, NEG)
    total[...] = jnp.zeros_like(total)
    acc[...] = jnp.zeros_like(acc)

    hidden_acc[...] = jnp.zeros_like(hidden_acc)
    build_gating()

    def second_third(j):
        second_step(j)
        third_step(j - 4)

    def third_project(j):
        third_step(j)
        project_step(j - 4)

    loop(second_third, 4, 8)
    loop(third_project, 4, 8)
    kv_wait(1, False)
    kv_third()
    loop(project_step, 4, 8)

    gate_proj = hidden_acc[0]
    active[0] = (gate_proj / (1.0 + jnp.exp(-gate_proj)) * hidden_acc[1]).astype(BF)
    down_copy.wait()

    def produce_step(j):
        o = order(j)
        @pl.when(jnp.logical_and(j > 0, j < 3))
        def _():
            back = jnp.where(rows_ref[pl.ds(o + 1, 1), :] == sublane, 1.0, 0.0).astype(BF)
            active[o] = jnp.dot(back, active[0], preferred_element_type=F32).astype(BF)

        wait_sent(1, j)
        span = pl.ds(pl.multiple_of(j * CHUNK, CHUNK), CHUNK)
        send[0, j] = jnp.dot(active[o], wd[:, span], preferred_element_type=F32).astype(BF)
        start_hop(3, j, o)

    loop(produce_step)

    lane_key = lax.broadcasted_iota(jnp.int32, (1, BLOCK), 1)
    key_pos = (
        ((z + 4 - (lane_key >> 8)) & 3) * 256
        + ((x + 4 - ((lane_key >> 6) & 3)) & 3) * 64
        + ((c + (lane_key >> 5)) & 1) * 32
        + (lane_key & 31)
    )
    factor = HEAD_WIDTH ** (-0.5) * 1.4426950408889634

    def attend(t):
        behind = lax.div(t, 4)
        s = lax.rem(lax.div(t, 2), 2)
        half = lax.rem(t, 2)

        def block(masked):
            block_keys = keys[s, behind].reshape(BLOCK, HEAD_WIDTH)
            block_values = values[s, behind].reshape(BLOCK, HEAD_WIDTH)
            for q in range(2):
                first = pl.multiple_of(half * 512 + q * 256, 256)
                span = pl.ds(first, 256)
                scores = lax.dot_general(
                    qd[s, span], block_keys, (((1,), (1,)), ((), ())),
                    preferred_element_type=F32,
                ) * factor
                if masked:
                    query_pos = lax.broadcasted_iota(jnp.int32, (256, 1), 0) + first
                    scores = jnp.where(key_pos <= query_pos, scores, NEG)
                best_old = best[s, span]
                best_new = jnp.maximum(best_old, jnp.max(scores, axis=-1, keepdims=True))
                weights = jnp.exp2(scores - best_new[:, :1])
                shrink = jnp.exp2(best_old - best_new)
                best[s, span] = best_new
                total[s, span] = total[s, span] * shrink + jnp.sum(
                    weights, axis=-1, keepdims=True
                )
                acc[s, span] = acc[s, span] * shrink + jnp.dot(
                    weights.astype(BF), block_values, preferred_element_type=F32
                )

        pl.when(behind == 0)(lambda: block(True))
        pl.when(jnp.logical_and(behind > 0, behind <= y))(lambda: block(False))

    def return_second_step(j):
        wait_hop(3, j)
        wait_sent(2, j)
        reorder(3, j, 2)
        start_hop(4, j, order(j))

        @pl.when(j == 1)
        def _():
            kv_wait(2, False)
            kv_fourth()

        @pl.when(j == 3)
        def _():
            kv_wait(3, False)

        @pl.when(j >= 4)
        def _():
            attend(j - 4)

    loop(return_second_step)

    def return_third_step(j):
        wait_hop(4, j)
        wait_sent(3, j)
        o = order(j)
        for half in range(2):
            span = pl.ds(half * (CHUNK // 2), CHUNK // 2)
            mixed = jnp.dot(gating[o], recv[3, j, :, span], preferred_element_type=F32)
            send[0, j, 0:256, span] = (mixed[:256] + mixed[256:]).astype(BF)
        start_hop(5, j, o)
        attend(j + 4)

    loop(return_third_step)

    def combine_step(j):
        wait_hop(5, j)
        span = pl.ds(pl.multiple_of(j * CHUNK, CHUNK), CHUNK)
        parts = [recv_last[j, k * 64:(k + 1) * 64].astype(F32) for k in range(4)]
        out_ref[:, span] += (parts[0] + parts[1]) + (parts[2] + parts[3])

        @pl.when(j < 4)
        def _():
            attend(j + 12)

    loop(combine_step)

    for s in range(2):
        for b in range(4):
            span = slice(b * 256, (b + 1) * 256)
            ctx_ref[s, span] = (acc[s, span] / total[s, span]).astype(BF)

    def drain_step(j):
        wait_sent(0, j)
        wait_sent(4, j)
        wait_sent(5, j)

    loop(drain_step)
    for o in range(3):
        gate_copy(o, 1, 3, at(dc=1)).wait_send()
    for step in range(4):
        kv_wait(step, True)


def tile_rows(array):
    parts = array.reshape(array.shape[0], 2, -1, 128).transpose(0, 2, 1, 3)
    return parts.reshape(-1, 128)


def finish_kernel(parted_ref, tokens_ref, ctx_ref, out_ref):
    row = lax.broadcasted_iota(jnp.int32, (256, 256), 0)
    col = lax.broadcasted_iota(jnp.int32, (256, 256), 1)
    together = (col == ((row & 1) * 128 + (row >> 1))).astype(BF)
    for b in range(8):
        span = slice(b * 128, (b + 1) * 128)
        both = jnp.concatenate([parted_ref[s, span] for s in range(2)], axis=0)
        ctx_ref[b * 256:(b + 1) * 256] = jnp.dot(
            together, both, preferred_element_type=F32
        ).astype(BF)
    tiles = (col == ((row & 63) >> 1) * 8 + (row & 1) * 4 + (row >> 6)).astype(BF)
    for b in range(8):
        block = jnp.concatenate(
            [tokens_ref[b * 8:(b + 1) * 8, n * 128:(n + 1) * 128] for n in range(32)], axis=0
        ).astype(BF)
        out_ref[b * 256:(b + 1) * 256] = jnp.dot(
            tiles, block, preferred_element_type=F32
        ).astype(BF)


def body(
    queries, key_rows, values, hidden, norm_gain, routes, route_gates, expert_home,
    w_gate, w_up, w_down,
):
    columns, rows = slot_tables()
    vmem = pl.BlockSpec(memory_space=pltpu.VMEM)
    hbm = pl.BlockSpec(memory_space=pl.ANY)
    block = (CHUNKS, SLOTS, CHUNK)
    parted, tokens = pl.pallas_call(
        kernel,
        out_shape=(
            jax.ShapeDtypeStruct((2, BLOCK, HEAD_WIDTH), BF),
            jax.ShapeDtypeStruct((TOKENS, WIDTH), F32),
        ),
        in_specs=[vmem] * 10 + [hbm] * 3,
        out_specs=(vmem, vmem),
        scratch_shapes=[
            pltpu.VMEM((2,) + block, BF),
            pltpu.VMEM((4,) + block, BF),
            pltpu.VMEM((CHUNKS, 4 * TOKENS, CHUNK), BF),
            pltpu.VMEM((CHUNKS, 4 * TOKENS, CHUNK), BF),
            pltpu.VMEM((2, 2, CHUNK, FF), BF),
            pltpu.VMEM((FF, WIDTH), BF),
            pltpu.VMEM((5, SLOTS, SLOTS), BF),
            pltpu.VMEM((CHUNKS, TOKENS, CHUNK), BF),
            pltpu.VMEM((3, SLOTS, 2 * TOKENS), BF),
            pltpu.VMEM((3, SLOTS, 2 * TOKENS), BF),
            pltpu.VMEM((3, SLOTS, 4 * TOKENS), BF),
            pltpu.VMEM((3, 8 * TOKENS, SLOTS), BF),
            pltpu.VMEM((2, SLOTS, FF), F32),
            pltpu.VMEM((SLOTS, CHUNK), BF),
            pltpu.VMEM((3, SLOTS, FF), BF),
            pltpu.VMEM((2, 2, 32, HEAD_WIDTH), BF),
            pltpu.VMEM((2, 2, 32, HEAD_WIDTH), BF),
            pltpu.VMEM((2, 4, 4, 4, 2, 32, HEAD_WIDTH), BF),
            pltpu.VMEM((2, 4, 4, 4, 2, 32, HEAD_WIDTH), BF),
            pltpu.VMEM((2, BLOCK, HEAD_WIDTH), BF),
            pltpu.VMEM((2, BLOCK, HEAD_WIDTH), F32),
            pltpu.VMEM((2, BLOCK, HEAD_WIDTH), F32),
            pltpu.VMEM((2, BLOCK, HEAD_WIDTH), F32),
            pltpu.SemaphoreType.DMA((6, CHUNKS)),
            pltpu.SemaphoreType.DMA((6, CHUNKS)),
            pltpu.SemaphoreType.DMA((3,)),
            pltpu.SemaphoreType.DMA((3,)),
            pltpu.SemaphoreType.DMA((3, 2)),
            pltpu.SemaphoreType.DMA((4, 2, 4)),
            pltpu.SemaphoreType.DMA((4, 2, 4)),
        ],
        compiler_params=pltpu.CompilerParams(
            collective_id=0, has_side_effects=True, vmem_limit_bytes=62 * 2**20
        ),
    )(
        queries.reshape(2 * BLOCK, HEAD_WIDTH),
        tile_rows(key_rows),
        tile_rows(values),
        tile_rows(hidden),
        norm_gain.reshape(1, WIDTH),
        routes.transpose(1, 2, 0).reshape(2 * TOPK, -1),
        route_gates.transpose(1, 2, 0).reshape(2 * TOPK, -1),
        expert_home.reshape(1, 128),
        jnp.asarray(columns),
        jnp.asarray(rows),
        w_gate[0],
        w_up[0],
        w_down[0],
    )
    context, layer_out = pl.pallas_call(
        finish_kernel,
        out_shape=(
            jax.ShapeDtypeStruct((2 * BLOCK, HEAD_WIDTH), BF),
            jax.ShapeDtypeStruct((TOKENS * WIDTH // 128, 128), BF),
        ),
        in_specs=[vmem, vmem],
        out_specs=(vmem, vmem),
    )(parted, tokens)
    layer_out = layer_out.reshape(-1, WIDTH // 128, 2, 128).transpose(0, 2, 1, 3)
    return context.reshape(queries.shape), layer_out.reshape(hidden.shape)


def solution(mesh):
    both = P(("ctx", "exp"), None, None)
    in_specs = (P("ctx", None, "exp"), both, both, both, P(), both, both, P(), both, both, both)
    out_specs = (P("ctx", None, "exp"), both)
    return jax.shard_map(body, mesh=mesh, in_specs=in_specs, out_specs=out_specs, check_vma=False)
```

time: 123 us -> 110 us (0.89)
  local copies, waits for them, and re-layouts: 13.3 us -> 0 us
    reshape x5 -> x0, local copies, waits for them, and re-layouts: 8.37 us -> none  [the longest x1 2.17 us: body(): return (context.reshape(queries.shape), layer_out.reshape(hidden.shape))]
    unnamed x3 -> x0, local copies, waits for them, and re-layouts: 4.98 us -> none
    pallas_call x1 -> x2, Pallas kernels: 108 us -> 109 us  [the longest x1 106 us: body(): pl.pallas_call(kernel, out_shape=(jax.ShapeDtypeStruct((2, BLOCK, HEAD_WI...]
where the time goes in v2:
time: 110 us
  Pallas kernels  109 us (99%)
    pallas_call x1, Pallas kernels, body(): pl.pallas_call(kernel, out_shape=(jax.ShapeDtypeStruct((2, BLOCK, HEAD_WI...  106 us
    pallas_call x1, Pallas kernels, body(): pl.pallas_call(finish_kernel, out_shape=(jax.ShapeDtypeStruct((2 * BLOCK,...  2.88 us

profile of v2, /device:TPU:25, one launch (start us, length us, event | category | flops | bytes accessed | tf_op | source)
XLA Modules:
  0.0 110.0 jit_solution(6085128347380813074)
XLA Ops:
  0.6 106.5 %shard_map.140 = (bf16[2,1024,128]{2,1,0:T(8,128)(2,1)}, f32[64,4096]{1,0:T(8,128)}) custom-call(bf16[2048,128]{1,0:T(8,128)(2,1)} %bitcast.36, bf16[128,128]{1,0:T(8,128)(2,1)} %bitcast.38, bf16[128,128]{1,0:T(8,128)(2,1)} %bitcast.39, bf16[2048,128]{1,0:T(8,128)(2,1)} %bitcast.37, f32[1,4096]{1,0:T(1,128)} %bitcast.40, s32[16,32]{1,0:T(8,128)} %bitcast.41, ...), custom_call_target="tpu_custom_call" | custom-call | tf_op jit(solution)/shard_map/pallas_call | solution.py:599
  107.1 2.9 %shard_map.141 = (bf16[2048,128]{1,0:T(8,128)(2,1)}, bf16[2048,128]{1,0:T(8,128)(2,1)}) custom-call(bf16[2,1024,128]{2,1,0:T(8,128)(2,1)} %get-tuple-element.6.parted_ref, f32[64,4096]{1,0:T(8,128)} %get-tuple-element.7.tokens_ref), custom_call_target="tpu_custom_call" | custom-call | tf_op jit(solution)/shard_map/pallas_call | solution.py:657

commit v3 on v2

--- a/solution.py
+++ b/solution.py
@@ -14,7 +14,7 @@
 CAP = 3
 TOKENS = 64
 SLOTS = 384
-CHUNKS = 8
+CHUNKS = 16
 CHUNK = WIDTH // CHUNKS
 BLOCK = 1024
 ORDERS = (("y", "z", "x"), ("z", "x", "y"), ("x", "y", "z"))
@@ -60,7 +60,7 @@
     ctx_ref, out_ref,
     send, recv, recv_first, recv_last, wgu, wd, perm, normed, gates_own, gates_all, placing,
     gating, hidden_acc, rows_in, active,
-    key_own, value_own, keys, values, qd, best, total, acc,
+    key_own, value_own, keys, values, qd,
     send_sem, recv_sem, gate_send, gate_recv, weight_sem, kv_send, kv_recv,
 ):
     y = lax.axis_index("ctx")
@@ -268,7 +268,7 @@
 
 
     kv_first()
-    loop(lambda j: start_hop(0, j, order(j)), 0, 4)
+    loop(lambda j: start_hop(0, j, order(j)), 0, 8)
 
     expert_row = lax.broadcasted_iota(jnp.int32, (128, 32), 0)
     picked_parts, gate_parts = [], []
@@ -327,7 +327,7 @@
         for k in (1, 2, 3):
             gate_copy(o, k, 1, at(**{"d" + ORDERS[o][0]: k})).start()
 
-    loop(lambda j: start_hop(0, j, order(j)), 4, 8)
+    loop(lambda j: start_hop(0, j, order(j)), 8, 16)
     kv_wait(0, False)
     kv_second()
 
@@ -338,8 +338,8 @@
     perm[2] = jnp.where(rows_ref[0:1, :] == sublane, 1.0, 0.0).astype(BF)
 
     def reorder(stage, j, matrix):
-        for half in range(2):
-            span = pl.ds(half * (CHUNK // 2), CHUNK // 2)
+        for half in range(1):
+            span = pl.ds(0, CHUNK)
             send[stage % 2, j, :, span] = jnp.dot(
                 perm[matrix], recv[stage - 1, j, :, span], preferred_element_type=F32
             ).astype(BF)
@@ -368,8 +368,8 @@
     def second_step(j):
         o = order(j)
         wait_hop(0, j)
-        for half in range(2):
-            span = pl.ds(half * (CHUNK // 2), CHUNK // 2)
+        for half in range(1):
+            span = pl.ds(0, CHUNK)
             send[0, j, :, span] = jnp.dot(
                 placing[o], recv_first[j, :, span], preferred_element_type=F32
             ).astype(BF)
@@ -410,7 +410,7 @@
             for copy in gate_up_copies(j + 2, slot):
                 copy.start()
 
-    loop(second_step, 0, 4)
+    loop(second_step, 0, 8)
 
     apart256 = (col256 == ((row256 & 127) * 2 + (row256 >> 7))).astype(BF)
     for b in range(8):
@@ -419,26 +419,23 @@
         ).astype(BF)
         for s in range(2):
             qd[s, b * 128:(b + 1) * 128] = parted[s * 128:(s + 1) * 128]
-    best[...] = jnp.full_like(best, NEG)
-    total[...] = jnp.zeros_like(total)
-    acc[...] = jnp.zeros_like(acc)
 
     hidden_acc[...] = jnp.zeros_like(hidden_acc)
     build_gating()
 
     def second_third(j):
         second_step(j)
-        third_step(j - 4)
+        third_step(j - 8)
 
     def third_project(j):
         third_step(j)
-        project_step(j - 4)
-
-    loop(second_third, 4, 8)
-    loop(third_project, 4, 8)
+        project_step(j - 8)
+
+    loop(second_third, 8, 16)
+    loop(third_project, 8, 16)
     kv_wait(1, False)
     kv_third()
-    loop(project_step, 4, 8)
+    loop(project_step, 8, 16)
 
     gate_proj = hidden_acc[0]
     active[0] = (gate_proj / (1.0 + jnp.exp(-gate_proj)) * hidden_acc[1]).astype(BF)
@@ -468,37 +465,28 @@
     factor = HEAD_WIDTH ** (-0.5) * 1.4426950408889634
 
     def attend(t):
-        behind = lax.div(t, 4)
-        s = lax.rem(lax.div(t, 2), 2)
-        half = lax.rem(t, 2)
-
-        def block(masked):
-            block_keys = keys[s, behind].reshape(BLOCK, HEAD_WIDTH)
-            block_values = values[s, behind].reshape(BLOCK, HEAD_WIDTH)
-            for q in range(2):
-                first = pl.multiple_of(half * 512 + q * 256, 256)
-                span = pl.ds(first, 256)
-                scores = lax.dot_general(
-                    qd[s, span], block_keys, (((1,), (1,)), ((), ())),
-                    preferred_element_type=F32,
-                ) * factor
-                if masked:
-                    query_pos = lax.broadcasted_iota(jnp.int32, (256, 1), 0) + first
-                    scores = jnp.where(key_pos <= query_pos, scores, NEG)
-                best_old = best[s, span]
-                best_new = jnp.maximum(best_old, jnp.max(scores, axis=-1, keepdims=True))
-                weights = jnp.exp2(scores - best_new[:, :1])
-                shrink = jnp.exp2(best_old - best_new)
-                best[s, span] = best_new
-                total[s, span] = total[s, span] * shrink + jnp.sum(
-                    weights, axis=-1, keepdims=True
-                )
-                acc[s, span] = acc[s, span] * shrink + jnp.dot(
-                    weights.astype(BF), block_values, preferred_element_type=F32
-                )
-
-        pl.when(behind == 0)(lambda: block(True))
-        pl.when(jnp.logical_and(behind > 0, behind <= y))(lambda: block(False))
+        s = lax.div(t, 4)
+        first = pl.multiple_of(lax.rem(t, 4) * 256, 256)
+        span = pl.ds(first, 256)
+
+        def rows(blocks):
+            seen_keys = keys[s, 0:blocks].reshape(blocks * BLOCK, HEAD_WIDTH)
+            seen_values = values[s, 0:blocks].reshape(blocks * BLOCK, HEAD_WIDTH)
+            scores = lax.dot_general(
+                qd[s, span], seen_keys, (((1,), (1,)), ((), ())), preferred_element_type=F32
+            )
+            query_pos = lax.broadcasted_iota(jnp.int32, (256, 1), 0) + first
+            own = jnp.where(key_pos <= query_pos, scores[:, :BLOCK], NEG)
+            scores = own if blocks == 1 else jnp.concatenate([own, scores[:, BLOCK:]], axis=1)
+            best = jnp.max(scores, axis=-1, keepdims=True) * factor
+            weights = jnp.exp2(scores * factor - best)
+            total = jnp.sum(weights, axis=-1, keepdims=True)
+            ctx_ref[s, span] = (
+                jnp.dot(weights.astype(BF), seen_values, preferred_element_type=F32) / total
+            ).astype(BF)
+
+        for n in range(4):
+            pl.when(y == n)(lambda: rows(n + 1))
 
     def return_second_step(j):
         wait_hop(3, j)
@@ -506,33 +494,15 @@
         reorder(3, j, 2)
         start_hop(4, j, order(j))
 
-        @pl.when(j == 1)
-        def _():
-            kv_wait(2, False)
-            kv_fourth()
-
-        @pl.when(j == 3)
-        def _():
-            kv_wait(3, False)
-
-        @pl.when(j >= 4)
-        def _():
-            attend(j - 4)
-
-    loop(return_second_step)
-
     def return_third_step(j):
         wait_hop(4, j)
         wait_sent(3, j)
         o = order(j)
-        for half in range(2):
-            span = pl.ds(half * (CHUNK // 2), CHUNK // 2)
+        for half in range(1):
+            span = pl.ds(0, CHUNK)
             mixed = jnp.dot(gating[o], recv[3, j, :, span], preferred_element_type=F32)
             send[0, j, 0:256, span] = (mixed[:256] + mixed[256:]).astype(BF)
         start_hop(5, j, o)
-        attend(j + 4)
-
-    loop(return_third_step)
 
     def combine_step(j):
         wait_hop(5, j)
@@ -540,16 +510,33 @@
         parts = [recv_last[j, k * 64:(k + 1) * 64].astype(F32) for k in range(4)]
         out_ref[:, span] += (parts[0] + parts[1]) + (parts[2] + parts[3])
 
-        @pl.when(j < 4)
+    def first_back(j):
+        return_second_step(j)
+
+        @pl.when(j == 4)
         def _():
-            attend(j + 12)
-
-    loop(combine_step)
-
-    for s in range(2):
-        for b in range(4):
-            span = slice(b * 256, (b + 1) * 256)
-            ctx_ref[s, span] = (acc[s, span] / total[s, span]).astype(BF)
+            kv_wait(2, False)
+            kv_fourth()
+
+        pl.when(j == 8)(lambda: kv_wait(3, False))
+        pl.when(jnp.logical_and(j >= 12, j < 13))(lambda: attend(j - 12))
+
+    loop(first_back)
+
+    def second_back(j):
+        return_third_step(j)
+        due = lax.rem(j, 4) == 0
+        pl.when(due)(lambda: attend(lax.div(j, 4) + 1))
+
+    loop(second_back)
+
+    loop(attend, 5, 7)
+
+    def third_back(j):
+        combine_step(j)
+        pl.when(jnp.logical_and(j >= 6, j < 7))(lambda: attend(j + 1))
+
+    loop(third_back)
 
     def drain_step(j):
         wait_sent(0, j)
@@ -625,9 +612,6 @@
             pltpu.VMEM((2, 4, 4, 4, 2, 32, HEAD_WIDTH), BF),
             pltpu.VMEM((2, 4, 4, 4, 2, 32, HEAD_WIDTH), BF),
             pltpu.VMEM((2, BLOCK, HEAD_WIDTH), BF),
-            pltpu.VMEM((2, BLOCK, HEAD_WIDTH), F32),
-            pltpu.VMEM((2, BLOCK, HEAD_WIDTH), F32),
-            pltpu.VMEM((2, BLOCK, HEAD_WIDTH), F32),
             pltpu.SemaphoreType.DMA((6, CHUNKS)),
             pltpu.SemaphoreType.DMA((6, CHUNKS)),
             pltpu.SemaphoreType.DMA((3,)),

time: 110 us -> 99.2 us (0.902)
  Pallas kernels: 109 us -> 98.3 us
    pallas_call x1, Pallas kernels: 106 us -> 95.4 us  [body(): pl.pallas_call(kernel, out_shape=(jax.ShapeDtypeStruct((2, BLOCK, HEAD_WI...]
where the time goes in v3:
time: 99.2 us; the launch traced here: 99 us
  Pallas kernels  98.3 us (99%)
    pallas_call x1, Pallas kernels, body(): pl.pallas_call(kernel, out_shape=(jax.ShapeDtypeStruct((2, BLOCK, HEAD_WI...  95.4 us
    pallas_call x1, Pallas kernels, body(): pl.pallas_call(finish_kernel, out_shape=(jax.ShapeDtypeStruct((2 * BLOCK,...  2.88 us

profile of v3, /device:TPU:25, one launch (start us, length us, event | category | flops | bytes accessed | tf_op | source)
XLA Modules:
  0.0 99.0 jit_solution(13153723835570773259)
XLA Ops:
  0.6 95.4 %shard_map.140 = (bf16[2,1024,128]{2,1,0:T(8,128)(2,1)}, f32[64,4096]{1,0:T(8,128)}) custom-call(bf16[2048,128]{1,0:T(8,128)(2,1)} %bitcast.36, bf16[128,128]{1,0:T(8,128)(2,1)} %bitcast.38, bf16[128,128]{1,0:T(8,128)(2,1)} %bitcast.39, bf16[2048,128]{1,0:T(8,128)(2,1)} %bitcast.37, f32[1,4096]{1,0:T(1,128)} %bitcast.40, s32[16,32]{1,0:T(8,128)} %bitcast.41, ...), custom_call_target="tpu_custom_call" | custom-call | tf_op jit(solution)/shard_map/pallas_call | solution.py:586
  96.1 2.9 %shard_map.141 = (bf16[2048,128]{1,0:T(8,128)(2,1)}, bf16[2048,128]{1,0:T(8,128)(2,1)}) custom-call(bf16[2,1024,128]{2,1,0:T(8,128)(2,1)} %get-tuple-element.6.parted_ref, f32[64,4096]{1,0:T(8,128)} %get-tuple-element.7.tokens_ref), custom_call_target="tpu_custom_call" | custom-call | tf_op jit(solution)/shard_map/pallas_call | solution.py:641

commit v4 on v3

--- a/solution.py
+++ b/solution.py
@@ -233,11 +233,11 @@
 
         def start(axis):
             if hop == 2:
-                for k in (4, 5, 2, 6, 3, 7, 1):
+                for k in (2, 6, 3, 7, 4, 5, 1):
                     device = at(**{axis: sign * (k // 2), "dc": k % 2})
                     piece(stage, j, k, 1, device).start()
             else:
-                for k in (2, 1, 3):
+                for k in (1, 3, 2):
                     piece(stage, j, k, 1, at(**{axis: sign * k})).start()
 
         along(o, hop, start)
@@ -513,24 +513,24 @@
     def first_back(j):
         return_second_step(j)
 
-        @pl.when(j == 4)
+        @pl.when(j == 2)
         def _():
             kv_wait(2, False)
             kv_fourth()
 
-        pl.when(j == 8)(lambda: kv_wait(3, False))
-        pl.when(jnp.logical_and(j >= 12, j < 13))(lambda: attend(j - 12))
+        pl.when(j == 6)(lambda: kv_wait(3, False))
+        pl.when(jnp.logical_or(j == 8, j == 12))(lambda: attend(lax.div(j, 4) - 2))
 
     loop(first_back)
 
     def second_back(j):
         return_third_step(j)
         due = lax.rem(j, 4) == 0
-        pl.when(due)(lambda: attend(lax.div(j, 4) + 1))
+        pl.when(due)(lambda: attend(lax.div(j, 4) + 2))
 
     loop(second_back)
 
-    loop(attend, 5, 7)
+    loop(attend, 6, 7)
 
     def third_back(j):
         combine_step(j)

time: 99.2 us -> 97.4 us (0.982)
  Pallas kernels: 98.3 us -> 96.5 us
    pallas_call x1, Pallas kernels: 95.4 us -> 93.6 us  [body(): pl.pallas_call(kernel, out_shape=(jax.ShapeDtypeStruct((2, BLOCK, HEAD_WI...]
where the time goes in v4:
time: 97.4 us; the launch traced here: 97.2 us
  Pallas kernels  96.5 us (99%)
    pallas_call x1, Pallas kernels, body(): pl.pallas_call(kernel, out_shape=(jax.ShapeDtypeStruct((2, BLOCK, HEAD_WI...  93.6 us
    pallas_call x1, Pallas kernels, body(): pl.pallas_call(finish_kernel, out_shape=(jax.ShapeDtypeStruct((2 * BLOCK,...  2.88 us

profile of v4, /device:TPU:25, one launch (start us, length us, event | category | flops | bytes accessed | tf_op | source)
XLA Modules:
  0.0 97.2 jit_solution(1535183205394071648)
XLA Ops:
  0.6 93.6 %shard_map.140 = (bf16[2,1024,128]{2,1,0:T(8,128)(2,1)}, f32[64,4096]{1,0:T(8,128)}) custom-call(bf16[2048,128]{1,0:T(8,128)(2,1)} %bitcast.36, bf16[128,128]{1,0:T(8,128)(2,1)} %bitcast.38, bf16[128,128]{1,0:T(8,128)(2,1)} %bitcast.39, bf16[2048,128]{1,0:T(8,128)(2,1)} %bitcast.37, f32[1,4096]{1,0:T(1,128)} %bitcast.40, s32[16,32]{1,0:T(8,128)} %bitcast.41, ...), custom_call_target="tpu_custom_call" | custom-call | tf_op jit(solution)/shard_map/pallas_call | solution.py:586
  94.3 2.9 %shard_map.141 = (bf16[2048,128]{1,0:T(8,128)(2,1)}, bf16[2048,128]{1,0:T(8,128)(2,1)}) custom-call(bf16[2,1024,128]{2,1,0:T(8,128)(2,1)} %get-tuple-element.6.parted_ref, f32[64,4096]{1,0:T(8,128)} %get-tuple-element.7.tokens_ref), custom_call_target="tpu_custom_call" | custom-call | tf_op jit(solution)/shard_map/pallas_call | solution.py:641
